TPU v7x, 32 devices: a whole 2x2x4 slice. The times are simulated.
32 devices in a mesh: grp: 4 (over y, x), tok: 4 (over z), mdl: 2 (over core).
Axes of the slice: x: 2, y: 2, z: 4, core: 2. Of those that a mesh axis runs over, the one named last changes fastest.
Arguments:
- hidden_in: bfloat16 [4, 512, 5120], P('grp', 'tok', 'mdl'), may hold values from -8 to 8
- seg_ids: int32 [4, 512], replicated, may hold values from 0 to 3, never falling along the last dimension, each value on 1 to 384 neighbouring positions
- request_prefix: int32 [4, 4], replicated, may hold values from 0 to 1
- page_table: int32 [32], replicated, may hold values from 0 to 31, each once
- prefix_cache: bfloat16 [32, 256, 8, 256], P(('grp', 'mdl'), None, 'tok'), may hold values from -200 to 200
- attn_gain: float32 [5120], P('mdl'), may hold values from 0.1 to 1.9
- w_query: bfloat16 [5120, 5120], P('mdl', 'tok'), may hold values from -0.078125 to 0.078125
- w_key: bfloat16 [5120, 1024], P('mdl', 'tok'), may hold values from -0.25 to 0.25
- w_value: bfloat16 [5120, 1024], P('mdl', 'tok'), may hold values from -0.078125 to 0.078125
- w_out: bfloat16 [5120, 5120], P('tok', 'mdl'), may hold values from -0.078125 to 0.078125
- ffn_gain: float32 [5120], P('mdl'), may hold values from 0.1 to 1.9
- w_gate: bfloat16 [5120, 14336], P('mdl', 'tok'), may hold values from -0.078125 to 0.078125
- w_up: bfloat16 [5120, 14336], P('mdl', 'tok'), may hold values from -0.078125 to 0.078125
- w_down: bfloat16 [14336, 5120], P('tok', 'mdl'), may hold values from -0.046875 to 0.046875
- final_gain: float32 [5120], replicated, may hold values from 0.1 to 1.9
- lm_head: bfloat16 [76800, 5120], P(('grp', 'tok', 'mdl')), may hold values from -0.25 to 0.25
Outputs:
- hidden_out: bfloat16 [4, 512, 5120], P('grp', 'tok', 'mdl')
- new_kv: bfloat16 [4, 512, 8, 256], P('grp', 'mdl', 'tok')
- req_norm: float32 [4, 4], P('grp')
- max_logit: float32 [4, 4], replicated
- logits: float32 [16, 76800], P(None, ('grp', 'tok', 'mdl'))
Inputs may be any that keep to these rules, and one draw needn't show every extreme that they name: `seg_ids`: requests of a group are contiguous, in order, and none is empty. `page_table`: each physical slot holds exactly one logical page.
All inputs are finite; a program needn't handle non-finite values.
Results may differ from a plain program's by a relative error of at most 0.024.
Values may be sent and summed in bfloat16 or wider, within the bound.
A program may use at most 256 MiB of HBM per device.

v0:
```python
import jax
import jax.numpy as jnp
from jax import lax
from jax.sharding import PartitionSpec as P

PREFIX = 4096
PAGE = 256


EPS = 1e-06
THETA = 1000000.0
NEG = -1e30


def rotate(tensor, positions):
    half_dim = tensor.shape[-1] // 2
    frequency = THETA ** (-(jnp.arange(half_dim, dtype=jnp.float32) * 2.0 / tensor.shape[-1]))
    angles = positions.astype(jnp.float32)[:, None] * frequency[None, :]
    cosine = jnp.cos(angles)[:, None, :]
    sine_part = jnp.sin(angles)[:, None, :]
    first_part = tensor[..., :half_dim]
    second = tensor[..., half_dim:]
    return jnp.concatenate(
        [first_part * cosine - second * sine_part, second * cosine + first_part * sine_part], -1
    )


def on_device(
    hidden_in,
    seg_ids,
    request_prefix,
    page_table,
    prefix_cache,
    attn_gain,
    w_query,
    w_key,
    w_value,
    w_out,
    ffn_gain,
    w_gate,
    w_up,
    w_down,
    final_gain,
    lm_head,
):
    groups_total = seg_ids.shape[0]
    seq_len = seg_ids.shape[1]
    req_count = request_prefix.shape[1]
    tok_rows = hidden_in.shape[1]
    feat_dev = hidden_in.shape[2]
    model_width = feat_dev * lax.axis_size("mdl")
    head_dim = prefix_cache.shape[3] // 2
    kv_dev = prefix_cache.shape[2]
    heads_dev = w_query.shape[1] // head_dim
    group_size = heads_dev // kv_dev
    page_len = prefix_cache.shape[1]
    slot_total = page_table.shape[0]
    rows_mdl = seq_len // lax.axis_size("mdl")
    group_idx = lax.axis_index("grp")
    tok_idx = lax.axis_index("tok")
    mdl_idx = lax.axis_index("mdl")
    score_scale = head_dim ** (-0.5)
    tokens = hidden_in[0].astype(jnp.float32)
    squares = lax.psum(jnp.sum(tokens * tokens, -1), "mdl")
    normed = (tokens * lax.rsqrt(squares[:, None] / model_width + EPS) * attn_gain).astype(
        jnp.bfloat16
    )
    w_joined = jnp.concatenate([w_query, w_key, w_value], 1)
    partial_qkv = jnp.dot(
        lax.all_gather(normed, "tok", axis=0, tiled=True),
        w_joined,
        preferred_element_type=jnp.float32,
    )
    qkv_rows = lax.psum_scatter(partial_qkv, "mdl", scatter_dimension=0, tiled=True)
    q_cols = heads_dev * head_dim
    kv_cols = kv_dev * head_dim
    queries = qkv_rows[:, :q_cols].reshape(rows_mdl, heads_dev, head_dim)
    key_rows = qkv_rows[:, q_cols : q_cols + kv_cols].reshape(rows_mdl, kv_dev, head_dim)
    value_rows = qkv_rows[:, q_cols + kv_cols :].reshape(rows_mdl, kv_dev, head_dim)
    seg_row = lax.dynamic_index_in_dim(seg_ids, group_idx, 0, keepdims=False)
    prefix_row = lax.dynamic_index_in_dim(request_prefix, group_idx, 0, keepdims=False)
    requests = jnp.arange(req_count, dtype=jnp.int32)
    member = seg_row[:, None] == requests[None, :]
    counts = jnp.sum(member.astype(jnp.int32), 0)
    offsets = jnp.cumsum(counts) - counts
    row_start = mdl_idx * rows_mdl
    my_rows = row_start + jnp.arange(rows_mdl, dtype=jnp.int32)
    my_seg = lax.dynamic_slice_in_dim(seg_row, row_start, rows_mdl)
    my_member = my_seg[:, None] == requests[None, :]
    positions = PREFIX + my_rows - jnp.sum(jnp.where(my_member, offsets[None, :], 0), 1)
    my_prefix = jnp.sum(jnp.where(my_member, prefix_row[None, :], 0), 1)
    q_rot = (
        rotate(queries, positions)
        .astype(jnp.bfloat16)
        .reshape(rows_mdl, kv_dev, group_size, head_dim)
    )
    k_rot = rotate(key_rows, positions).astype(jnp.bfloat16)
    appended = jnp.concatenate([k_rot, value_rows.astype(jnp.bfloat16)], -1)
    suffix = lax.all_gather(appended, "mdl", axis=0, tiled=True)
    every_row = jnp.arange(seq_len, dtype=jnp.int32)
    suffix_ok = ((seg_row[None, :] == my_seg[:, None]) & (every_row[None, :] <= my_rows[:, None]))[
        :, None, None, :
    ]
    suffix_scores = (
        jnp.einsum(
            "rcgd,tcd->rcgt", q_rot, suffix[..., :head_dim], preferred_element_type=jnp.float32
        )
        * score_scale
    )
    suffix_scores = jnp.where(suffix_ok, suffix_scores, NEG)
    row_max = jnp.max(suffix_scores, -1)
    suffix_weights = jnp.where(suffix_ok, jnp.exp(suffix_scores - row_max[..., None]), 0.0)
    row_total = jnp.sum(suffix_weights, -1)
    mixed = jnp.einsum(
        "rcgt,tcd->rcgd",
        suffix_weights.astype(jnp.bfloat16),
        suffix[..., head_dim:],
        preferred_element_type=jnp.float32,
    )
    slot_ids = jnp.arange(slot_total, dtype=jnp.int32)
    pages_each = PREFIX // PAGE
    slot_prefix = jnp.sum(
        jnp.where(page_table[None, :] == slot_ids[:, None], (slot_ids // pages_each)[None, :], 0), 1
    )
    piece = lax.all_gather(prefix_cache, ("grp", "mdl"), axis=0, tiled=True)
    page_count = piece.shape[0]
    key_prefix = jnp.repeat(slot_prefix, page_len)
    allowed = (my_prefix[:, None] == key_prefix[None, :])[:, None, None, :]
    flat_pages = piece.reshape(page_count * page_len, kv_dev, 2 * head_dim)
    scores = (
        jnp.einsum(
            "rcgd,kcd->rcgk", q_rot, flat_pages[..., :head_dim], preferred_element_type=jnp.float32
        )
        * score_scale
    )
    scores = jnp.where(allowed, scores, NEG)
    new_max = jnp.maximum(row_max, jnp.max(scores, -1))
    factor = jnp.exp(row_max - new_max)
    page_weights = jnp.where(allowed, jnp.exp(scores - new_max[..., None]), 0.0)
    new_total = row_total * factor + jnp.sum(page_weights, -1)
    new_mixed = mixed * factor[..., None] + jnp.einsum(
        "rcgk,kcd->rcgd",
        page_weights.astype(jnp.bfloat16),
        flat_pages[..., head_dim:],
        preferred_element_type=jnp.float32,
    )
    attended = (
        (new_mixed / new_total[..., None])
        .astype(jnp.bfloat16)
        .reshape(rows_mdl, heads_dev * head_dim)
    )
    partial_out = jnp.dot(
        lax.all_gather(attended, "mdl", axis=0, tiled=True),
        w_out,
        preferred_element_type=jnp.float32,
    )
    residual = tokens + lax.psum_scatter(
        partial_out.astype(jnp.bfloat16), "tok", scatter_dimension=0, tiled=True
    ).astype(jnp.float32)
    squares_ffn = lax.psum(jnp.sum(residual * residual, -1), "mdl")
    ffn_input = (residual * lax.rsqrt(squares_ffn[:, None] / model_width + EPS) * ffn_gain).astype(
        jnp.bfloat16
    )
    w_pair = jnp.concatenate([w_gate, w_up], 1)
    ff_dev = w_gate.shape[1]
    partial_ffn = jnp.dot(
        lax.all_gather(ffn_input, "tok", axis=0, tiled=True),
        w_pair,
        preferred_element_type=jnp.float32,
    )
    summed = lax.psum_scatter(
        partial_ffn.astype(jnp.bfloat16), "mdl", scatter_dimension=0, tiled=True
    ).astype(jnp.float32)
    activated = (jax.nn.silu(summed[:, :ff_dev]) * summed[:, ff_dev:]).astype(jnp.bfloat16)
    partial_down = jnp.dot(
        lax.all_gather(activated, "mdl", axis=0, tiled=True),
        w_down,
        preferred_element_type=jnp.float32,
    )
    final_rows = residual + lax.psum_scatter(
        partial_down.astype(jnp.bfloat16), "tok", scatter_dimension=0, tiled=True
    ).astype(jnp.float32)
    tok_start = tok_idx * tok_rows
    my_tok_rows = tok_start + jnp.arange(tok_rows, dtype=jnp.int32)
    tok_seg = lax.dynamic_slice_in_dim(seg_row, tok_start, tok_rows)
    row_squares = jnp.sum(final_rows * final_rows, -1)
    req_squares = jnp.sum(
        jnp.where(tok_seg[:, None] == requests[None, :], row_squares[:, None], 0.0), 0
    )
    ends = offsets + counts - 1
    picked = ends[:, None] == my_tok_rows[None, :]
    last_part = jnp.sum(jnp.where(picked[:, :, None], final_rows[None, :, :], 0.0), 1)
    padded = jnp.zeros((groups_total * req_count, model_width), jnp.float32)
    padded = lax.dynamic_update_slice(
        padded, last_part, (group_idx * req_count, mdl_idx * feat_dev)
    )
    req_total = lax.psum(req_squares, ("tok", "mdl"))
    last_all = lax.psum(padded, ("grp", "tok", "mdl"))
    req_norm = jnp.sqrt(req_total / (counts.astype(jnp.float32) * model_width) + EPS)
    last_normed = (
        last_all * lax.rsqrt(jnp.mean(last_all * last_all, -1, keepdims=True) + EPS) * final_gain
    ).astype(jnp.bfloat16)
    logits = lax.dot_general(
        last_normed, lm_head, (((1,), (1,)), ((), ())), preferred_element_type=jnp.float32
    )
    max_logit = lax.pmax(jnp.max(logits, -1), ("grp", "tok", "mdl")).reshape(
        groups_total, req_count
    )
    return (
        final_rows.astype(jnp.bfloat16)[None],
        appended[None],
        req_norm[None],
        max_logit,
        logits,
    )


def solution(mesh):
    return jax.shard_map(
        on_device,
        mesh=mesh,
        in_specs=(
            P("grp", "tok", "mdl"),
            P(),
            P(),
            P(),
            P(("grp", "mdl"), None, "tok", None),
            P("mdl"),
            P("mdl", "tok"),
            P("mdl", "tok"),
            P("mdl", "tok"),
            P("tok", "mdl"),
            P("mdl"),
            P("mdl", "tok"),
            P("mdl", "tok"),
            P("tok", "mdl"),
            P(),
            P(("grp", "tok", "mdl"), None),
        ),
        out_specs=(
            P("grp", "tok", "mdl"),
            P("grp", "mdl", "tok", None),
            P("grp", None),
            P(),
            P(None, ("grp", "tok", "mdl")),
        ),
        check_vma=False,
    )
```

profile of v0, /device:TPU:0, one launch (start us, length us, event | category | flops | bytes accessed | tf_op | source)
XLA Modules:
  0.0 698.7 jit_solution(7826711781206043604)
XLA Ops:
  8.1 1.3 fusion.41
  9.4 2.6 psum.28
  12.0 2.1 fusion.43
  14.2 57.5 %all-gather.6.cloned.1.call-done = bf16[512,2560]{1,0:T(8,128)(2,1)} async-done(((bf16[128,2560]{1,0:T(8,128)(2,1)}), bf16[512,2560]{1,0:T(8,128)(2,1)}) %all-gather.6.cloned.1.call-update) | async-done | bytes 2621456 | tf_op jit(solution)/shard_map/all_gather | solution.py:70
  71.7 10.4 %fusion.15 = f32[512,1792]{1,0:T(8,128)} fusion(bf16[512,2560]{1,0:T(8,128)(2,1)} %all-gather.6.cloned.1.call-done, bf16[2560,256]{1,0:T(8,128)(2,1)} %param.24, bf16[2560,256]{1,0:T(8,128)(2,1)} %param.23, bf16[2560,1280]{1,0:T(8,128)(2,1)} %param.22), kind=kOutput, calls=%fused_computation.15 | convolution fusion | flops 4725145600 | bytes 15466496 | tf_op jit(solution)/shard_map/dot_general | solution.py:69
  82.2 1.1 copy.82
  83.4 0.7 constant_dynamic-slice_fusion
  84.6 0.8 dynamic_slice.14
  85.4 0.5 bitcast_add_fusion
  86.0 0.3 multiply_cosine_fusion
  86.4 0.8 copy.73
  87.1 0.8 copy.75
  88.1 1.2 broadcast_compare_fusion
  89.3 3.3 reduce-scatter.5.cloned.1.call-done
  92.6 2.6 slice.59
  95.2 1.7 copy.77
  96.9 1.9 subtract_convert_fusion
  98.9 1.3 copy.78
  100.2 1.3 copy.79
  101.5 1.7 slice.53
  103.2 1.8 reshape.290
  104.9 1.0 copy_bitcast_fusion
  105.9 1.4 fusion.62
  107.3 1.1 subtract_convert_fusion.1
  108.6 2.2 all_gather.19
  110.8 0.8 copy-done.6
  111.5 1.3 fusion.21
  112.9 2.4 copy-done.2
  115.3 1.8 fusion.23
  117.1 20.6 %all-gather.8.cloned.1.call-done = bf16[32,256,2,256]{3,1,2,0:T(8,128)(2,1)} async-done(((bf16[4,256,2,256]{3,1,2,0:T(8,128)(2,1)}), bf16[32,256,2,256]{3,1,2,0:T(8,128)(2,1)}) %all-gather.8.cloned.1.call-update) | async-done | bytes 8388624 | tf_op jit(solution)/shard_map/all_gather | solution.py:125
  137.7 7.6 %copy.83 = bf16[32,256,2,256]{3,1,0,2:T(8,128)(2,1)} copy(bf16[32,256,2,256]{3,1,2,0:T(8,128)(2,1)} %all-gather.8.cloned.1.call-done) | data formatting | bytes 16777216 | tf_op jit(solution)/shard_map/all_gather | solution.py:125
  145.3 32.9 %bitcast_reduce_fusion = (f32[256,2,5]{0,2,1:T(8,128)}, f32[2,256,5,8192]{3,1,2,0:T(8,128)}) fusion(pred[256,8192]{1,0:T(8,128)(4,1)S(1)} %broadcast_compare_fusion, bf16[8192,2,256]{2,0,1:T(8,128)(2,1)} %bitcast.117, bf16[256,2,5,64]{3,0,2,1:T(8,128)(2,1)S(1)} %bitcast.123, bf16[256,2,5,64]{3,0,2,1:T(8,128)(2,1)S(1)} %bitcast.121), kind=kOutput, calls=%fused_computation.1 | convolution fusion | flops 5432931840 | bytes 90843136 | tf_op jit(solution)/shard_map/rcgd,kcd->rcgk/dot_general | solution.py:131
  178.2 0.7 max.15
  178.9 28.9 %fusion.2 = f32[256,2,5]{0,2,1:T(8,128)S(1)} fusion(f32[2,256,5,8192]{3,1,2,0:T(8,128)} %get-tuple-element.49, f32[256,2,5]{0,2,1:T(8,128)S(1)} %max.15, pred[256,8192]{1,0:T(8,128)(4,1)S(1)} %broadcast_compare_fusion), kind=kLoop, calls=%fused_computation.5 | loop fusion | flops 104855040 | bytes 86003712 | tf_op jit(solution)/shard_map/reduce_sum | solution.py:140
  207.9 5.0 fusion.38
  212.9 32.3 %divide_convert_fusion = bf16[256,2,5,128]{0,3,2,1:T(8,128)(2,1)} fusion(f32[256,2,5,128]{0,3,2,1:T(8,128)} %fusion.38, bf16[8192,2,256]{2,0,1:T(8,128)(2,1)} %bitcast.118, f32[2,256,5,8192]{3,1,2,0:T(8,128)} %get-tuple-element.49, f32[256,2,5]{0,2,1:T(8,128)S(1)} %max.15, pred[256,8192]{1,0:T(8,128)(4,1)S(1)} %broadcast_compare_fusion, ...), kind=kOutput, calls=%fused_computation.51 | convolution fusion | flops 5474549760 | bytes 94273536 | tf_op jit(solution)/shard_map/rcgk,kcd->rcgd/dot_general | solution.py:141
  245.5 9.2 %all-gather.10.cloned.1.call-done = bf16[512,1280]{0,1:T(8,128)(2,1)} async-done(((bf16[256,1280]{0,1:T(8,128)(2,1)}), bf16[512,1280]{0,1:T(8,128)(2,1)}) %all-gather.10.cloned.1.call-update) | async-done | bytes 1310736 | tf_op jit(solution)/shard_map/all_gather | solution.py:153
  254.7 8.4 %convolution_convert_fusion.1 = bf16[512,2560]{1,0:T(8,128)(2,1)} fusion(bf16[512,1280]{0,1:T(8,128)(2,1)} %all-gather.10.cloned.1.call-done, bf16[1280,2560]{1,0:T(8,128)(2,1)} %param.25), kind=kOutput, calls=%fused_computation.26 | convolution fusion | flops 3356753920 | bytes 10485760 | tf_op jit(solution)/shard_map/dot_general | solution.py:152
  263.2 53.4 %reduce-scatter.7.cloned.1.call-done = bf16[128,2560]{1,0:T(8,128)(2,1)} async-done(((bf16[512,2560]{1,0:T(8,128)(2,1)}), bf16[128,2560]{1,0:T(8,128)(2,1)}) %reduce-scatter.7.cloned.1.call-update) | async-done | bytes 655376 | tf_op jit(solution)/shard_map/reduce_scatter | solution.py:157
  316.6 1.4 multiply_reduce_fusion.1
  318.0 2.5 psum.29
  320.5 2.2 multiply_convert_fusion
  322.7 54.6 %all-gather.12.cloned.1.call-done = bf16[512,2560]{1,0:T(8,128)(2,1)} async-done(((bf16[128,2560]{1,0:T(8,128)(2,1)}), bf16[512,2560]{1,0:T(8,128)(2,1)}) %all-gather.12.cloned.1.call-update) | async-done | bytes 2621456 | tf_op jit(solution)/shard_map/all_gather | solution.py:167
  377.3 25.7 %fusion.12 = bf16[512,7168]{1,0:T(8,128)(2,1)} fusion(bf16[512,2560]{1,0:T(8,128)(2,1)} %all-gather.12.cloned.1.call-done, bf16[2560,3584]{1,0:T(8,128)(2,1)} %param.28, bf16[2560,3584]{1,0:T(8,128)(2,1)} %param.27), kind=kOutput, calls=%fused_computation.14 | convolution fusion | flops 18867552256 | bytes 46661632 | tf_op jit(solution)/shard_map/dot_general | solution.py:166
  403.2 14.7 %reduce-scatter.9.cloned.1.call-done = bf16[256,7168]{1,0:T(8,128)(2,1)} async-done(((bf16[512,7168]{1,0:T(8,128)(2,1)}), bf16[256,7168]{1,0:T(8,128)(2,1)}) %reduce-scatter.9.cloned.1.call-update) | async-done | bytes 3670032 | tf_op jit(solution)/shard_map/reduce_scatter | solution.py:171
  417.9 2.9 convert_element_type.82
  420.8 2.3 fusion.25
  423.2 0.3 reduce-scatter.11.cloned.1.call-start
  423.5 13.9 %all-gather.14.cloned.1.call-done = bf16[512,3584]{1,0:T(8,128)(2,1)} async-done(((bf16[256,3584]{1,0:T(8,128)(2,1)}), bf16[512,3584]{1,0:T(8,128)(2,1)}) %all-gather.14.cloned.1.call-update) | async-done | bytes 3670032 | tf_op jit(solution)/shard_map/all_gather | solution.py:176
  437.3 15.6 %convolution_convert_fusion = bf16[512,2560]{1,0:T(8,128)(2,1)} fusion(bf16[512,3584]{1,0:T(8,128)(2,1)} %all-gather.14.cloned.1.call-done, bf16[3584,2560]{1,0:T(8,128)(2,1)} %param.29), kind=kOutput, calls=%fused_computation.25 | convolution fusion | flops 9396551680 | bytes 24641536 | tf_op jit(solution)/shard_map/dot_general | solution.py:175
  453.0 0.8 dynamic-slice_bitcast_fusion
  454.0 1.0 copy.85
  455.0 51.4 %reduce-scatter.11.cloned.1.call-done = bf16[128,2560]{1,0:T(8,128)(2,1)} async-done(((bf16[512,2560]{1,0:T(8,128)(2,1)}), bf16[128,2560]{1,0:T(8,128)(2,1)}) %reduce-scatter.11.cloned.1.call-update) | async-done | bytes 655376 | tf_op jit(solution)/shard_map/reduce_scatter | solution.py:180
  506.4 1.5 multiply_reduce_fusion
  507.9 0.7 select_reduce_fusion
  508.7 1.6 dynamic_update_slice.3
  510.3 0.7 copy-done.5
  511.1 0.9 convert_bitcast_fusion
  512.0 14.5 %psum.30 = f32[4]{0:T(128)S(1)} all-reduce(f32[4]{0:T(128)S(1)} %select_reduce_fusion.4), channel_id=1, replica_groups=mesh['grp'=4,'tok'=4,'mdl'=2] {'tok','mdl'}, use_global_device_ids=true, to_apply=%region_19.20 | all-reduce | flops 4 | bytes 32 | tf_op jit(solution)/shard_map/psum | solution.py:197
  526.6 109.1 %all-reduce.2.cloned.1.call-done = f32[16,5120]{1,0:T(8,128)} async-done(((f32[16,5120]{1,0:T(8,128)}), f32[16,5120]{1,0:T(8,128)}) %all-reduce.2.cloned.1.call-update) | async-done | bytes 327696 | tf_op jit(solution)/shard_map/psum | solution.py:198
  635.6 1.1 multiply_reduce_fusion.2
  636.8 12.2 %fusion.63 = (f32[16]{0:T(128)S(1)}, f32[16,2400]{1,0:T(8,128)}) fusion(bf16[2400,5120]{1,0:T(8,128)(2,1)} %param.31, f32[16,5120]{1,0:T(8,128)} %all-reduce.2.cloned.1.call-done, f32[5120]{0:T(1024)S(1)} %copy-done.19, f32[16]{0:T(128)S(1)} %add_rsqrt_fusion), kind=kOutput, calls=%fused_computation.116 | convolution fusion | flops 393500160 | bytes 25077888 | tf_op jit(solution)/shard_map/dot_general | solution.py:203
  649.1 0.5 sqrt_bitcast_fusion
  649.7 41.2 %pmax.7 = f32[4,4]{1,0:T(4,128)} all-reduce(f32[4,4]{1,0:T(4,128)S(1)} %reshape.296), channel_id=1, replica_groups=mesh['grp'=4,'tok'=4,'mdl'=2] {'grp','tok','mdl'}, use_global_device_ids=true, to_apply=%region_24.25 | all-reduce | flops 16 | bytes 128 | tf_op jit(solution)/shard_map/pmax | solution.py:206
  (91 shorter events, 2.3 us)
Async XLA Ops:
  8.0 77.4 %copy-start = (s32[4,4]{1,0:T(4,128)S(1)}, s32[4,4]{1,0:T(4,128)}, u32[]{:S(2)}) copy-start(s32[4,4]{1,0:T(4,128)} %param.18) | copy-start | bytes 196
  8.0 63.7 %all-gather.6.cloned.1.call-start = ((), (), s32[]{:S(2)}) async-start(), calls=%async_computation.4 | async-start | bytes 3276800 | tf_op jit(solution)/shard_map/all_gather | solution.py:70
  14.1 68.1 %copy-start.14 = (bf16[4,256,2,256]{3,2,1,0:T(2,128)(2,1)S(1)}, bf16[4,256,2,256]{3,2,1,0:T(2,128)(2,1)}, u32[]{:S(2)}) copy-start(bf16[4,256,2,256]{3,2,1,0:T(2,128)(2,1)} %param.20) | copy-start | bytes 3145732
  14.1 78.5 %reduce-scatter.5.cloned.1.call-start = ((), (), s32[]{:S(2)}) async-start(), calls=%async_computation.5 | async-start | bytes 5505024 | tf_op jit(solution)/shard_map/reduce_scatter | solution.py:74
  82.1 2.3 copy-start.25
  82.1 55.6 %all-gather.8.cloned.1.call-start = ((), (), s32[]{:S(2)}) async-start(), calls=%async_computation.6 | async-start | bytes 9437184 | tf_op jit(solution)/shard_map/all_gather | solution.py:125
  83.3 171.4 %all-gather.10.cloned.1.call-start = ((), (), s32[]{:S(2)}) async-start(), calls=%async_computation.7 | async-start | bytes 1966080 | tf_op jit(solution)/shard_map/all_gather | solution.py:153
  84.2 1.8 copy-start.22
  86.4 1.7 copy-start.15
  86.4 1.7 copy-start.16
  105.9 4.8 copy-start.8
  108.4 2.4 copy-start.10
  108.4 2.4 copy-start.12
  110.8 0.8 copy-start.6
  112.8 2.4 copy-start.2
  112.9 2.4 copy-start.17
  178.9 28.9 %copy-start.18 = (f32[256,2,5]{0,2,1:T(8,128)S(1)}, f32[256,2,5]{0,2,1:T(8,128)}, u32[]{:S(2)}) copy-start(f32[256,2,5]{0,2,1:T(8,128)} %copy-done.17) | copy-start | bytes 30724
  178.9 28.9 %copy-start.20 = (f32[256,2,5]{0,2,1:T(8,128)S(1)}, f32[256,2,5]{0,2,1:T(8,128)}, u32[]{:S(2)}) copy-start(f32[256,2,5]{0,2,1:T(8,128)} %fusion.23) | copy-start | bytes 30724
  178.9 29.0 %copy-start.7 = (bf16[512,2,256]{2,0,1:T(8,128)(2,1)S(1)}, bf16[512,2,256]{2,0,1:T(8,128)(2,1)}, u32[]{:S(2)}) copy-start(bf16[512,2,256]{2,0,1:T(8,128)(2,1)} %copy-done.6) | copy-start | bytes 1572868
  245.3 71.3 %copy-start.3 = (bf16[1,128,2560]{2,1,0:T(8,128)(2,1)S(1)}, bf16[1,128,2560]{2,1,0:T(8,128)(2,1)}, u32[]{:S(2)}) copy-start(bf16[1,128,2560]{2,1,0:T(8,128)(2,1)} %param.16) | copy-start | bytes 1966084
  245.3 75.2 %copy-start.21 = (f32[2560]{0:T(1024)S(1)}, f32[2560]{0:T(1024)}, u32[]{:S(2)}) copy-start(f32[2560]{0:T(1024)} %param.26) | copy-start | bytes 30724
  245.3 71.3 %reduce-scatter.7.cloned.1.call-start = ((), (), s32[]{:S(2)}) async-start(), calls=%async_computation.8 | async-start | bytes 3276800 | tf_op jit(solution)/shard_map/reduce_scatter | solution.py:157
  263.1 114.2 %all-gather.12.cloned.1.call-start = ((), (), s32[]{:S(2)}) async-start(), calls=%async_computation.9 | async-start | bytes 3276800 | tf_op jit(solution)/shard_map/all_gather | solution.py:167
  322.7 95.2 %reduce-scatter.9.cloned.1.call-start = ((), (), s32[]{:S(2)}) async-start(), calls=%async_computation.10 | async-start | bytes 11010048 | tf_op jit(solution)/shard_map/reduce_scatter | solution.py:171
  403.1 34.2 %all-gather.14.cloned.1.call-start = ((), (), s32[]{:S(2)}) async-start(), calls=%async_computation.11 | async-start | bytes 5505024 | tf_op jit(solution)/shard_map/all_gather | solution.py:176
  423.1 30.7 %copy-start.24 = (s32[4]{0:T(128)S(1)}, s32[4]{0:T(128)}, u32[]{:S(2)}) copy-start(s32[4]{0:T(128)} %get-tuple-element.44) | copy-start | bytes 52
  423.1 30.7 %copy-start.9 = (bf16[256,2,128]{2,0,1:T(8,128)(2,1)S(1)}, bf16[256,2,128]{2,0,1:T(8,128)(2,1)}, u32[]{:S(2)}) copy-start(bf16[256,2,128]{2,0,1:T(8,128)(2,1)} %copy-done.8) | copy-start | bytes 393220
  423.1 30.7 %copy-start.11 = (bf16[256,2,64]{2,0,1:T(8,128)(2,1)S(1)}, bf16[256,2,64]{2,0,1:T(8,128)(2,1)}, u32[]{:S(2)}) copy-start(bf16[256,2,64]{2,0,1:T(8,128)(2,1)} %copy-done.10) | copy-start | bytes 196612
  423.1 30.7 %copy-start.13 = (bf16[256,2,64]{2,0,1:T(8,128)(2,1)S(1)}, bf16[256,2,64]{2,0,1:T(8,128)(2,1)}, u32[]{:S(2)}) copy-start(bf16[256,2,64]{2,0,1:T(8,128)(2,1)} %copy-done.12) | copy-start | bytes 196612
  423.2 83.3 %copy-start.4 = (bf16[128,2560]{1,0:T(8,128)(2,1)S(1)}, bf16[128,2560]{1,0:T(8,128)(2,1)}, u32[]{:S(2)}) copy-start(bf16[128,2560]{1,0:T(8,128)(2,1)} %reduce-scatter.7.cloned.1.call-done) | copy-start | bytes 1966084
  423.2 83.3 %reduce-scatter.11.cloned.1.call-start = ((), (), s32[]{:S(2)}) async-start(), calls=%async_computation.12 | async-start | bytes 3276800 | tf_op jit(solution)/shard_map/reduce_scatter | solution.py:180
  452.9 183.8 %copy-start.19 = (f32[5120]{0:T(1024)S(1)}, f32[5120]{0:T(1024)}, u32[]{:S(2)}) copy-start(f32[5120]{0:T(1024)} %param.30) | copy-start | bytes 61444
  452.9 182.7 %all-reduce.2.cloned.1.call-start = ((), (), s32[]{:S(2)}) async-start(), calls=%async_computation.13 | async-start | bytes 655360 | tf_op jit(solution)/shard_map/psum | solution.py:198
  510.3 0.7 copy-start.5
  636.8 12.3 %copy-start.23 = (s32[4]{0:T(128)S(1)}, s32[4]{0:T(128)}, u32[]{:S(2)}) copy-start(s32[4]{0:T(128)} %copy-done.22) | copy-start | bytes 52
  636.8 54.1 %copy-start.1 = (s32[4,4]{1,0:T(4,128)S(1)}, s32[4,4]{1,0:T(4,128)}, u32[]{:S(2)}) copy-start(s32[4,4]{1,0:T(4,128)} %param.18) | copy-start | bytes 196
Sparse Core Ops, SparseCore 0:
  14.2 57.3 all-gather.5
  82.2 10.3 reduce-scatter.4
  245.4 9.3 all-gather.9
  263.3 53.2 reduce-scatter.6
  322.8 54.4 all-gather.11
  403.2 14.6 reduce-scatter.8
  423.2 14.0 all-gather.13
  453.1 53.3 reduce-scatter.10
Sparse Core Ops, SparseCore 1:
  84.6 53.0 all-gather.7
  511.1 124.5 all-reduce.1
where the time goes:
time: 708 us; the launch traced here: 699 us
  waiting for transfers between devices  388 us (55%)
  matrix products  144 us (20%)
  blocking collectives  62.9 us (9%)
  other arithmetic  54.7 us (8%)
  local copies, waits for them, and re-layouts  32 us (5%)
  between operations  16.4 us (2%)
    psum x1, waiting for transfers between devices, on_device(): last_all = lax.psum(padded, ('grp', 'tok', 'mdl'))  109 us
    all_gather x1, waiting for transfers between devices, on_device(): lax.all_gather(normed, 'tok', axis=0, tiled=True)  57.5 us
    all_gather x1, waiting for transfers between devices, on_device(): lax.all_gather(ffn_input, 'tok', axis=0, tiled=True)  54.6 us
    reduce_scatter x1, waiting for transfers between devices, on_device(): lax.psum_scatter(partial_out.astype(jnp.bfloat16), 'tok', scatter_dimensi...  53.4 us
    reduce_scatter x1, waiting for transfers between devices, on_device(): lax.psum_scatter(partial_down.astype(jnp.bfloat16), 'tok', scatter_dimens...  51.4 us
    pmax x1, blocking collectives, on_device(): lax.pmax(jnp.max(logits, -1), ('grp', 'tok', 'mdl'))  41.2 us
    dot_general x1, matrix products, on_device(): jnp.einsum('rcgd,kcd->rcgk', q_rot, flat_pages[..., :head_dim], preferred...  32.9 us
    dot_general x1, matrix products, on_device(): jnp.einsum('rcgk,kcd->rcgd', page_weights.astype(jnp.bfloat16), flat_page...  32.3 us
  transfers between devices with their start and end apart: 10, of which 10 were waited for; matrix products, arithmetic and copies ran while one was open for 4% of the time, Pallas kernels for 0%

commit v1 on v0

v1 whole, which is shorter than its diff:
```python
import functools

import jax
import jax.numpy as jnp
from jax import lax
from jax.experimental import pallas as pl
from jax.experimental.pallas import tpu as pltpu
from jax.sharding import PartitionSpec as P

PREFIX = 4096
PAGE = 256


EPS = 1e-06
THETA = 1000000.0
NEG = -1e30


MESH = pl.DeviceIdType.MESH
LOG2E = 1.4426950408889634


def turn(block, cosine, signed_sine):
    return block * cosine + pltpu.roll(block, block.shape[1] // 2, 1) * signed_sine


def rope_kv_body(k_ref, v_ref, cos_ref, sin_ref, out_ref):
    width = k_ref.shape[1]
    out_ref[:, :width] = turn(k_ref[...], cos_ref[...], sin_ref[...]).astype(jnp.bfloat16)
    out_ref[:, width:] = v_ref[...].astype(jnp.bfloat16)


def rope_kv(qkv_rows, cosine, sine, heads, kv_dev, head_dim):
    rows = qkv_rows.shape[0]
    return pl.pallas_call(
        rope_kv_body,
        grid=(kv_dev,),
        in_specs=[
            pl.BlockSpec((rows, head_dim), lambda c: (0, heads + c)),
            pl.BlockSpec((rows, head_dim), lambda c: (0, heads + kv_dev + c)),
            pl.BlockSpec((rows, head_dim), lambda c: (0, 0)),
            pl.BlockSpec((rows, head_dim), lambda c: (0, 0)),
        ],
        out_specs=pl.BlockSpec((rows, 2 * head_dim), lambda c: (0, c)),
        out_shape=jax.ShapeDtypeStruct((rows, kv_dev * 2 * head_dim), jnp.bfloat16),
    )(qkv_rows, qkv_rows, cosine, sine)


def attend_body(
    prefixes, pages_each, page_len, group_size, head_dim, together,
    table_ref, need_ref,
    q_ref, cos_ref, sin_ref, seg_ref, row_ref, prefix_ref, key_seg_ref, suffix_ref, pages_ref,
    out_ref,
):
    block = pl.program_id(1)
    toks = q_ref.shape[0]
    scale = head_dim ** (-0.5) * LOG2E
    contract = (((1,), (1,)), ((), ()))
    q = jnp.concatenate(
        [
            turn(q_ref[:, h * head_dim : (h + 1) * head_dim], cos_ref[...], sin_ref[...])
            for h in range(group_size)
        ],
        0,
    ).astype(jnp.bfloat16)
    stack = lambda column: jnp.concatenate([column] * group_size, 0)
    seg = stack(seg_ref[...])
    row = stack(row_ref[...])
    prefix = stack(prefix_ref[...])

    def fold(parts, op):
        width = head_dim
        pieces = [p[:, j : j + width] for p in parts for j in range(0, p.shape[1], width)]
        return functools.reduce(op, pieces)

    keys = suffix_ref[:, :head_dim]
    scores = lax.dot_general(q, keys, contract, preferred_element_type=jnp.float32) * scale
    index = lax.broadcasted_iota(jnp.int32, scores.shape, 1)
    scores = jnp.where((key_seg_ref[...] == seg) & (index <= row), scores, NEG)
    top = jnp.max(fold([scores], jnp.maximum), 1, keepdims=True)
    weights = jnp.exp2(scores - top)
    total = fold([weights], jnp.add)
    mixed = jnp.dot(
        weights.astype(jnp.bfloat16), suffix_ref[:, head_dim:], preferred_element_type=jnp.float32
    )
    for p in range(prefixes):
        seen = prefix == p

        def step(i, carry):
            top, total, mixed = carry
            starts = [
                pl.multiple_of(
                    table_ref[p * pages_each + i * together + u] * page_len, page_len
                )
                for u in range(together)
            ]
            scores = [
                lax.dot_general(
                    q,
                    pages_ref[pl.ds(start, page_len), :head_dim],
                    contract,
                    preferred_element_type=jnp.float32,
                )
                for start in starts
            ]
            best = jnp.max(fold(scores, jnp.maximum), 1, keepdims=True) * scale
            new_top = jnp.where(seen, jnp.maximum(top, best), top)
            shift = jnp.where(seen, new_top, -NEG)
            factor = jnp.exp2(top - new_top)
            weights = [jnp.exp2(s * scale - shift) for s in scores]
            total = total * factor + fold(weights, jnp.add)
            mixed = mixed * factor
            for start, w in zip(starts, weights):
                mixed = mixed + jnp.dot(
                    w.astype(jnp.bfloat16),
                    pages_ref[pl.ds(start, page_len), head_dim:],
                    preferred_element_type=jnp.float32,
                )
            return new_top, total, mixed

        trips = need_ref[block * prefixes + p] * (pages_each // together)
        top, total, mixed = lax.fori_loop(0, trips, step, (top, total, mixed))
    result = (mixed / jnp.sum(total, 1, keepdims=True)).astype(jnp.bfloat16)
    for h in range(group_size):
        out_ref[:, h * head_dim : (h + 1) * head_dim] = result[h * toks : (h + 1) * toks]


def attend(
    qkv_rows, cosine, sine, my_seg, my_rows, my_prefix, seg_row, suffix, pages, page_table,
    kv_dev, group_size, head_dim, page_len,
):
    rows = qkv_rows.shape[0]
    toks = 64
    blocks = rows // toks
    pages_each = PREFIX // PAGE
    prefixes = page_table.shape[0] // pages_each
    need = jnp.max(
        (my_prefix.reshape(blocks, toks)[:, None, :] == jnp.arange(prefixes)[None, :, None]).astype(
            jnp.int32
        ),
        -1,
    ).reshape(-1)
    seq_len = suffix.shape[0]
    q_width = group_size * head_dim
    by_row = lambda c, b, *_: (b, 0)
    by_kv = lambda c, b, *_: (0, c)
    by_both = lambda c, b, *_: (b, c)
    body = functools.partial(
        attend_body, prefixes, pages_each, page_len, group_size, head_dim, 4
    )
    elements = rows * kv_dev * group_size * (PREFIX + seq_len)
    return pl.pallas_call(
        body,
        grid_spec=pltpu.PrefetchScalarGridSpec(
            num_scalar_prefetch=2,
            grid=(kv_dev, blocks),
            in_specs=[
                pl.BlockSpec((toks, q_width), by_both),
                pl.BlockSpec((toks, head_dim), by_row),
                pl.BlockSpec((toks, head_dim), by_row),
                pl.BlockSpec((toks, 1), by_row),
                pl.BlockSpec((toks, 1), by_row),
                pl.BlockSpec((toks, 1), by_row),
                pl.BlockSpec((1, seq_len), lambda c, b, *_: (0, 0)),
                pl.BlockSpec((seq_len, 2 * head_dim), by_kv),
                pl.BlockSpec((pages.shape[0], 2 * head_dim), by_kv),
            ],
            out_specs=pl.BlockSpec((toks, q_width), by_both),
        ),
        out_shape=jax.ShapeDtypeStruct((rows, kv_dev * q_width), jnp.bfloat16),
        compiler_params=pltpu.CompilerParams(vmem_limit_bytes=48 * 1024 * 1024),
        cost_estimate=pl.CostEstimate(
            flops=4 * head_dim * elements, bytes_accessed=pages.size * 2, transcendentals=elements
        ),
    )(
        page_table, need, qkv_rows, cosine, sine, my_seg[:, None], my_rows[:, None],
        my_prefix[:, None], seg_row[None, :], suffix, pages,
    )


def exchange_body(
    sizes, summing,
    x_ref, out_ref, tok_slots, stage, all_slots, tok_send, tok_recv, all_send, all_recv,
):
    grp_n, tok_n, mdl_n = sizes
    g, t, m = (lax.axis_index(name) for name in ("grp", "tok", "mdl"))
    tok_peers = [
        (d, {"tok": lax.rem(t + d, tok_n)}) for d in range(1, tok_n)
    ]
    plane_peers = [
        (
            gd * mdl_n + md,
            {"grp": lax.rem(g + gd, grp_n), "mdl": lax.rem(m + md, mdl_n)},
        )
        for gd in range(grp_n)
        for md in range(mdl_n)
        if gd + md > 0
    ]
    barrier = pltpu.get_barrier_semaphore()
    for _, peer in tok_peers + plane_peers:
        pl.semaphore_signal(barrier, inc=1, device_id=peer, device_id_type=MESH)
    pl.semaphore_wait(barrier, len(tok_peers) + len(plane_peers))

    def spread(source, slots, mine, peers, send, recv):
        copies = [
            pltpu.make_async_remote_copy(
                src_ref=source,
                dst_ref=slots.at[mine],
                send_sem=send.at[d],
                recv_sem=recv.at[d],
                device_id=peer,
                device_id_type=MESH,
            )
            for d, peer in peers
        ]
        for copy in copies:
            copy.start()
        slots[mine] = source[...]
        for copy in copies:
            copy.wait()

    join = jnp.add if summing else jnp.maximum
    spread(x_ref, tok_slots, t, tok_peers, tok_send, tok_recv)
    stage[...] = functools.reduce(join, [tok_slots[k] for k in range(tok_n)])
    spread(stage, all_slots, g * mdl_n + m, plane_peers, all_send, all_recv)
    if summing:
        out_ref[...] = all_slots[...]
    else:
        out_ref[...] = functools.reduce(join, [all_slots[k] for k in range(grp_n * mdl_n)])


def exchange(values, summing):
    sizes = tuple(lax.axis_size(name) for name in ("grp", "tok", "mdl"))
    plane = sizes[0] * sizes[2]
    shape = values.shape
    return pl.pallas_call(
        functools.partial(exchange_body, sizes, summing),
        out_shape=jax.ShapeDtypeStruct((plane,) + shape if summing else shape, jnp.float32),
        in_specs=[pl.BlockSpec(memory_space=pltpu.VMEM)],
        out_specs=pl.BlockSpec(memory_space=pltpu.VMEM),
        scratch_shapes=[
            pltpu.VMEM((sizes[1],) + shape, jnp.float32),
            pltpu.VMEM(shape, jnp.float32),
            pltpu.VMEM((plane,) + shape, jnp.float32),
            pltpu.SemaphoreType.DMA((sizes[1],)),
            pltpu.SemaphoreType.DMA((sizes[1],)),
            pltpu.SemaphoreType.DMA((plane,)),
            pltpu.SemaphoreType.DMA((plane,)),
        ],
        compiler_params=pltpu.CompilerParams(
            collective_id=1 if summing else 2, has_side_effects=True
        ),
    )(values)


def on_device(
    hidden_in,
    seg_ids,
    request_prefix,
    page_table,
    prefix_cache,
    attn_gain,
    w_query,
    w_key,
    w_value,
    w_out,
    ffn_gain,
    w_gate,
    w_up,
    w_down,
    final_gain,
    lm_head,
):
    groups_total = seg_ids.shape[0]
    seq_len = seg_ids.shape[1]
    req_count = request_prefix.shape[1]
    tok_rows = hidden_in.shape[1]
    feat_dev = hidden_in.shape[2]
    model_width = feat_dev * lax.axis_size("mdl")
    head_dim = prefix_cache.shape[3] // 2
    kv_dev = prefix_cache.shape[2]
    heads_dev = w_query.shape[1] // head_dim
    group_size = heads_dev // kv_dev
    page_len = prefix_cache.shape[1]
    rows_mdl = seq_len // lax.axis_size("mdl")
    group_idx = lax.axis_index("grp")
    tok_idx = lax.axis_index("tok")
    mdl_idx = lax.axis_index("mdl")
    tokens = hidden_in[0].astype(jnp.float32)
    squares = lax.psum(jnp.sum(tokens * tokens, -1), "mdl")
    normed = (tokens * lax.rsqrt(squares[:, None] / model_width + EPS) * attn_gain).astype(
        jnp.bfloat16
    )
    w_joined = jnp.concatenate([w_query, w_key, w_value], 1)
    partial_qkv = jnp.dot(
        lax.all_gather(normed, "tok", axis=0, tiled=True),
        w_joined,
        preferred_element_type=jnp.float32,
    )
    pages = lax.all_gather(
        prefix_cache.reshape(-1, kv_dev * 2 * head_dim), ("grp", "mdl"), axis=0, tiled=True
    )
    partial_qkv, pages = lax.optimization_barrier((partial_qkv, pages))
    qkv_rows = lax.psum_scatter(partial_qkv, "mdl", scatter_dimension=0, tiled=True)
    seg_row = lax.dynamic_index_in_dim(seg_ids, group_idx, 0, keepdims=False)
    prefix_row = lax.dynamic_index_in_dim(request_prefix, group_idx, 0, keepdims=False)
    requests = jnp.arange(req_count, dtype=jnp.int32)
    member = seg_row[:, None] == requests[None, :]
    counts = jnp.sum(member.astype(jnp.int32), 0)
    offsets = jnp.cumsum(counts) - counts
    row_start = mdl_idx * rows_mdl
    my_rows = row_start + jnp.arange(rows_mdl, dtype=jnp.int32)
    my_seg = lax.dynamic_slice_in_dim(seg_row, row_start, rows_mdl)
    my_member = my_seg[:, None] == requests[None, :]
    positions = PREFIX + my_rows - jnp.sum(jnp.where(my_member, offsets[None, :], 0), 1)
    my_prefix = jnp.sum(jnp.where(my_member, prefix_row[None, :], 0), 1)
    frequency = THETA ** (
        -(jnp.arange(head_dim // 2, dtype=jnp.float32) * 2.0 / head_dim)
    )
    angles = positions.astype(jnp.float32)[:, None] * frequency[None, :]
    cosine = jnp.cos(angles)
    sine = jnp.sin(angles)
    cosine = jnp.concatenate([cosine, cosine], 1)
    sine = jnp.concatenate([-sine, sine], 1)
    appended = rope_kv(qkv_rows, cosine, sine, heads_dev, kv_dev, head_dim)
    suffix = lax.all_gather(appended, "mdl", axis=0, tiled=True)
    attended = attend(
        qkv_rows, cosine, sine, my_seg, my_rows, my_prefix, seg_row, suffix, pages, page_table,
        kv_dev, group_size, head_dim, page_len,
    )
    partial_out = jnp.dot(
        lax.all_gather(attended, "mdl", axis=0, tiled=True),
        w_out,
        preferred_element_type=jnp.float32,
    )
    residual = tokens + lax.psum_scatter(
        partial_out.astype(jnp.bfloat16), "tok", scatter_dimension=0, tiled=True
    ).astype(jnp.float32)
    squares_ffn = lax.psum(jnp.sum(residual * residual, -1), "mdl")
    ffn_input = (residual * lax.rsqrt(squares_ffn[:, None] / model_width + EPS) * ffn_gain).astype(
        jnp.bfloat16
    )
    w_pair = jnp.concatenate([w_gate, w_up], 1)
    ff_dev = w_gate.shape[1]
    partial_ffn = jnp.dot(
        lax.all_gather(ffn_input, "tok", axis=0, tiled=True),
        w_pair,
        preferred_element_type=jnp.float32,
    )
    summed = lax.psum_scatter(
        partial_ffn.astype(jnp.bfloat16), "mdl", scatter_dimension=0, tiled=True
    ).astype(jnp.float32)
    activated = (jax.nn.silu(summed[:, :ff_dev]) * summed[:, ff_dev:]).astype(jnp.bfloat16)
    partial_down = jnp.dot(
        lax.all_gather(activated, "mdl", axis=0, tiled=True),
        w_down,
        preferred_element_type=jnp.float32,
    )
    final_rows = residual + lax.psum_scatter(
        partial_down.astype(jnp.bfloat16), "tok", scatter_dimension=0, tiled=True
    ).astype(jnp.float32)
    tok_start = tok_idx * tok_rows
    my_tok_rows = tok_start + jnp.arange(tok_rows, dtype=jnp.int32)
    tok_seg = lax.dynamic_slice_in_dim(seg_row, tok_start, tok_rows)
    row_squares = jnp.sum(final_rows * final_rows, -1)
    req_squares = jnp.sum(
        jnp.where(tok_seg[:, None] == requests[None, :], row_squares[:, None], 0.0), 0
    )
    ends = offsets + counts - 1
    picked = ends[:, None] == my_tok_rows[None, :]
    last_part = jnp.sum(jnp.where(picked[:, :, None], final_rows[None, :, :], 0.0), 1)
    half = req_count * feat_dev // 8
    width = -(-half // 128) * 128
    bundle = jnp.concatenate(
        [
            jnp.pad(last_part.reshape(8, half), ((0, 0), (0, width - half))),
            jnp.pad(req_squares[:, None], ((0, 8 - req_count), (0, 127))),
        ],
        1,
    )
    everyone = exchange(bundle, True)
    mdl_total = lax.axis_size("mdl")
    last_all = (
        everyone[:, :, :half]
        .reshape(groups_total, mdl_total, req_count, feat_dev)
        .transpose(0, 2, 1, 3)
        .reshape(groups_total * req_count, model_width)
    )
    squares_all = everyone[:, :req_count, width].reshape(groups_total, mdl_total, req_count)
    req_total = lax.dynamic_index_in_dim(jnp.sum(squares_all, 1), group_idx, 0, keepdims=False)
    req_norm = jnp.sqrt(req_total / (counts.astype(jnp.float32) * model_width) + EPS)
    last_normed = (
        last_all * lax.rsqrt(jnp.mean(last_all * last_all, -1, keepdims=True) + EPS) * final_gain
    ).astype(jnp.bfloat16)
    logits = lax.dot_general(
        last_normed, lm_head, (((1,), (1,)), ((), ())), preferred_element_type=jnp.float32
    )
    rows_all = groups_total * req_count
    best = jnp.broadcast_to(jnp.max(logits, -1)[:, None], (rows_all, 128))
    max_logit = exchange(best, False)[:, 0].reshape(groups_total, req_count)
    return (
        final_rows.astype(jnp.bfloat16)[None],
        appended.reshape(1, rows_mdl, kv_dev, 2 * head_dim),
        req_norm[None],
        max_logit,
        logits,
    )


def solution(mesh):
    return jax.shard_map(
        on_device,
        mesh=mesh,
        in_specs=(
            P("grp", "tok", "mdl"),
            P(),
            P(),
            P(),
            P(("grp", "mdl"), None, "tok", None),
            P("mdl"),
            P("mdl", "tok"),
            P("mdl", "tok"),
            P("mdl", "tok"),
            P("tok", "mdl"),
            P("mdl"),
            P("mdl", "tok"),
            P("mdl", "tok"),
            P("tok", "mdl"),
            P(),
            P(("grp", "tok", "mdl"), None),
        ),
        out_specs=(
            P("grp", "tok", "mdl"),
            P("grp", "mdl", "tok", None),
            P("grp", None),
            P(),
            P(None, ("grp", "tok", "mdl")),
        ),
        check_vma=False,
    )
```

time: 708 us -> 519 us (0.73); the launches traced: 699 us -> 518 us
  Pallas kernels: 0 us -> 76.6 us
  matrix products: 144 us -> 72.3 us
  waiting for transfers between devices: 388 us -> 319 us
  blocking collectives: 62.9 us -> 7.43 us
  other arithmetic: 54.7 us -> 19.1 us
  local copies, waits for them, and re-layouts: 32 us -> 8.64 us
    psum x1 -> x0, waiting for transfers between devices: 109 us -> none  [on_device(): last_all = lax.psum(padded, ('grp', 'tok', 'mdl'))]
    pallas_call x0 -> x4, Pallas kernels: none -> 76.6 us  [the longest x1 48.6 us: attend(): pl.pallas_call(body, grid_spec=pltpu.PrefetchScalarGridSpec(num_scalar_pr...]
    dot_general x4 -> x0, matrix products: 71.5 us -> none  [the longest x1 32.9 us: on_device(): jnp.einsum('rcgd,kcd->rcgk', q_rot, flat_pages[..., :head_dim], preferred...]
    pmax x1 -> x0, blocking collectives: 41.2 us -> none  [on_device(): lax.pmax(jnp.max(logits, -1), ('grp', 'tok', 'mdl'))]
    reduce_sum x4 -> x2, other arithmetic: 31 us -> 0.11 us  [the longest x1 0.09 us: on_device(): jnp.sum(jnp.where(my_member, offsets[None, :], 0), 1)]
    all_gather x1, waiting for transfers between devices: 20.6 us -> 44.6 us  [on_device(): lax.all_gather(prefix_cache.reshape(-1, kv_dev * 2 * head_dim), ('grp', '...]
    psum x1 -> x0, blocking collectives: 14.5 us -> none  [on_device(): req_total = lax.psum(req_squares, ('tok', 'mdl'))]
    all_gather x1, waiting for transfers between devices: 9.2 us -> 19.2 us  [on_device(): lax.all_gather(attended, 'mdl', axis=0, tiled=True)]
  transfers between devices with their start and end apart: 10 -> 9, of which waited for: 10 -> 9; matrix products, arithmetic and copies ran while one was open for 4% -> 3% of each run, Pallas kernels for 0% -> 0%
where the time goes in v1:
time: 519 us; the launch traced here: 518 us
  waiting for transfers between devices  319 us (61%)
  Pallas kernels  76.6 us (15%)
  matrix products  72.3 us (14%)
  other arithmetic  19.1 us (4%)
  between operations  14.1 us (3%)
  local copies, waits for them, and re-layouts  8.64 us (2%)
  blocking collectives  7.43 us (1%)
    all_gather x1, waiting for transfers between devices, on_device(): lax.all_gather(normed, 'tok', axis=0, tiled=True)  55 us
    all_gather x1, waiting for transfers between devices, on_device(): lax.all_gather(ffn_input, 'tok', axis=0, tiled=True)  54.4 us
    reduce_scatter x1, waiting for transfers between devices, on_device(): lax.psum_scatter(partial_out.astype(jnp.bfloat16), 'tok', scatter_dimensi...  53.4 us
    reduce_scatter x1, waiting for transfers between devices, on_device(): lax.psum_scatter(partial_down.astype(jnp.bfloat16), 'tok', scatter_dimens...  52.5 us
    pallas_call x1, Pallas kernels, attend(): pl.pallas_call(body, grid_spec=pltpu.PrefetchScalarGridSpec(num_scalar_pr...  48.6 us
    all_gather x1, waiting for transfers between devices, on_device(): lax.all_gather(prefix_cache.reshape(-1, kv_dev * 2 * head_dim), ('grp', '...  44.6 us
    pallas_call x2, Pallas kernels, exchange(): pl.pallas_call(functools.partial(exchange_body, sizes, summing), out_shap...  25.9 us
    dot_general x1, matrix products, on_device(): jnp.dot(lax.all_gather(ffn_input, 'tok', axis=0, tiled=True), w_pair, pre...  25.7 us
  transfers between devices with their start and end apart: 9, of which 9 were waited for; matrix products, arithmetic and copies ran while one was open for 3% of the time, Pallas kernels for 0%

profile of v1, /device:TPU:0, one launch (start us, length us, event | category | flops | bytes accessed | tf_op | source)
XLA Modules:
  0.0 517.8 jit_solution(3107510428760442069)
XLA Ops:
  7.2 1.5 fusion.14
  8.7 2.6 psum.14
  11.3 2.1 fusion.16
  13.5 0.0 all-gather.8.cloned.1.call-start
  13.5 2.4 copy.31
  16.0 55.0 %all-gather.6.cloned.1.call-done = bf16[512,2560]{1,0:T(8,128)(2,1)} async-done(((bf16[128,2560]{1,0:T(8,128)(2,1)}), bf16[512,2560]{1,0:T(8,128)(2,1)}) %all-gather.6.cloned.1.call-update) | async-done | bytes 2621456 | tf_op jit(solution)/shard_map/all_gather | solution.py:296
  71.0 10.5 %fusion.7 = f32[512,1792]{1,0:T(8,128)} fusion(bf16[512,2560]{1,0:T(8,128)(2,1)} %all-gather.6.cloned.1.call-done, bf16[2560,256]{1,0:T(8,128)(2,1)S(1)} %copy-done.12, bf16[2560,256]{1,0:T(8,128)(2,1)S(1)} %copy-done.13, bf16[2560,1280]{1,0:T(8,128)(2,1)} %param.22), kind=kOutput, calls=%fused_computation.5 | convolution fusion | flops 4725145600 | bytes 15466496 | tf_op jit(solution)/shard_map/dot_general | solution.py:295
  81.5 44.6 %all-gather.8.cloned.1.call-done.pages_ref = bf16[8192,512]{1,0:T(8,128)(2,1)} async-done(((bf16[1024,512]{1,0:T(8,128)(2,1)}), bf16[8192,512]{1,0:T(8,128)(2,1)}) %all-gather.8.cloned.1.call-update) | async-done | bytes 8388624 | tf_op jit(solution)/shard_map/all_gather | solution.py:300
  126.2 0.1 convert_reduce_fusion
  126.3 0.2 reduce-window.7
  126.5 0.1 dynamic_slice.18
  126.6 0.1 select_reduce_fusion.1
  126.7 0.1 eq.81
  126.8 0.1 convert_reduce_fusion.1
  126.9 0.1 copy.26
  127.0 0.1 reshape.160.need_ref
  127.1 0.1 dynamic-slice_bitcast_fusion.1
  127.2 0.1 copy.27.seg_ref
  127.3 0.1 copy.28.prefix_ref
  127.5 0.5 fusion.21
  128.0 0.8 pad_maximum_fusion
  128.9 11.0 %reduce-scatter.5.cloned.1.call-done.k_ref.v_ref.q_ref = f32[256,1792]{1,0:T(8,128)} async-done(((f32[512,1792]{1,0:T(8,128)}), f32[256,1792]{1,0:T(8,128)}) %reduce-scatter.5.cloned.1.call-update) | async-done | bytes 1835024 | tf_op jit(solution)/shard_map/reduce_scatter | solution.py:304
  139.9 2.1 shard_map.191
  142.0 2.4 all_gather.20.suffix_ref
  144.4 48.6 %shard_map.192 = bf16[256,1280]{1,0:T(8,128)(2,1)} custom-call(s32[32]{0:T(128)S(1)} %copy-done.5, s32[8]{0:T(128)S(1)} %reshape.160.need_ref, f32[256,1792]{1,0:T(8,128)S(1)} %copy-done.2, f32[256,128]{1,0:T(8,128)S(1)} %copy-done.3, f32[256,128]{1,0:T(8,128)S(1)} %copy-done.4, s32[256,1]{1,0:T(8,128)S(1)} %copy.27.seg_ref, ...), custom_call_target="tpu_custom_call" | custom-call | flops 6039797760 | bytes 8388608 | tf_op jit(solution)/shard_map/pallas_call | solution.py:152
  193.1 19.2 %all-gather.10.cloned.1.call-done = bf16[512,1280]{1,0:T(8,128)(2,1)} async-done(((bf16[256,1280]{1,0:T(8,128)(2,1)}), bf16[512,1280]{1,0:T(8,128)(2,1)}) %all-gather.10.cloned.1.call-update) | async-done | bytes 1310736 | tf_op jit(solution)/shard_map/all_gather | solution.py:332
  212.3 8.3 %convolution_convert_fusion.1 = bf16[512,2560]{1,0:T(8,128)(2,1)} fusion(bf16[512,1280]{1,0:T(8,128)(2,1)} %all-gather.10.cloned.1.call-done, bf16[1280,2560]{1,0:T(8,128)(2,1)} %param.25), kind=kOutput, calls=%fused_computation.13 | convolution fusion | flops 3356753920 | bytes 10485760 | tf_op jit(solution)/shard_map/dot_general | solution.py:331
  220.7 53.4 %reduce-scatter.7.cloned.1.call-done = bf16[128,2560]{1,0:T(8,128)(2,1)} async-done(((bf16[512,2560]{1,0:T(8,128)(2,1)}), bf16[128,2560]{1,0:T(8,128)(2,1)}) %reduce-scatter.7.cloned.1.call-update) | async-done | bytes 655376 | tf_op jit(solution)/shard_map/reduce_scatter | solution.py:336
  274.1 1.4 multiply_reduce_fusion.1
  275.5 2.5 psum.15
  278.0 2.2 multiply_convert_fusion
  280.2 0.2 reduce-scatter.9.cloned.1.call-start
  280.4 54.4 %all-gather.12.cloned.1.call-done = bf16[512,2560]{1,0:T(8,128)(2,1)} async-done(((bf16[128,2560]{1,0:T(8,128)(2,1)}), bf16[512,2560]{1,0:T(8,128)(2,1)}) %all-gather.12.cloned.1.call-update) | async-done | bytes 2621456 | tf_op jit(solution)/shard_map/all_gather | solution.py:346
  334.8 25.7 %fusion.4 = bf16[512,7168]{1,0:T(8,128)(2,1)} fusion(bf16[512,2560]{1,0:T(8,128)(2,1)} %all-gather.12.cloned.1.call-done, bf16[2560,3584]{1,0:T(8,128)(2,1)} %param.28, bf16[2560,3584]{1,0:T(8,128)(2,1)} %param.27), kind=kOutput, calls=%fused_computation.4 | convolution fusion | flops 18867552256 | bytes 46661632 | tf_op jit(solution)/shard_map/dot_general | solution.py:345
  360.6 14.8 %reduce-scatter.9.cloned.1.call-done = bf16[256,7168]{1,0:T(8,128)(2,1)} async-done(((bf16[512,7168]{1,0:T(8,128)(2,1)}), bf16[256,7168]{1,0:T(8,128)(2,1)}) %reduce-scatter.9.cloned.1.call-update) | async-done | bytes 3670032 | tf_op jit(solution)/shard_map/reduce_scatter | solution.py:350
  375.4 2.9 convert_element_type.75
  378.3 2.3 fusion.13
  380.6 0.3 reduce-scatter.11.cloned.1.call-start
  380.9 13.9 %all-gather.14.cloned.1.call-done = bf16[512,3584]{1,0:T(8,128)(2,1)} async-done(((bf16[256,3584]{1,0:T(8,128)(2,1)}), bf16[512,3584]{1,0:T(8,128)(2,1)}) %all-gather.14.cloned.1.call-update) | async-done | bytes 3670032 | tf_op jit(solution)/shard_map/all_gather | solution.py:355
  394.8 15.7 %convolution_convert_fusion = bf16[512,2560]{1,0:T(8,128)(2,1)} fusion(bf16[512,3584]{1,0:T(8,128)(2,1)} %all-gather.14.cloned.1.call-done, bf16[3584,2560]{1,0:T(8,128)(2,1)} %param.29), kind=kOutput, calls=%fused_computation.12 | convolution fusion | flops 9396551680 | bytes 24641536 | tf_op jit(solution)/shard_map/dot_general | solution.py:354
  410.5 0.1 dynamic-slice_bitcast_fusion
  410.6 0.1 broadcast_compare_fusion
  410.7 0.8 reshape.164
  411.4 52.5 %reduce-scatter.11.cloned.1.call-done = bf16[128,2560]{1,0:T(8,128)(2,1)} async-done(((bf16[512,2560]{1,0:T(8,128)(2,1)}), bf16[128,2560]{1,0:T(8,128)(2,1)}) %reduce-scatter.11.cloned.1.call-update) | async-done | bytes 655376 | tf_op jit(solution)/shard_map/reduce_scatter | solution.py:359
  463.9 1.5 multiply_reduce_fusion
  465.4 0.9 convert_bitcast_fusion
  466.3 0.1 select_reduce_fusion.3
  466.5 0.1 copy.29
  466.5 0.7 select_reduce_fusion
  467.3 0.6 select_maximum_fusion.x_ref
  467.9 14.9 %shard_map.193 = f32[8,8,1408]{2,1,0:T(8,128)} custom-call(f32[8,1408]{1,0:T(8,128)} %select_maximum_fusion.x_ref), custom_call_target="tpu_custom_call" | custom-call | tf_op jit(solution)/shard_map/pallas_call | solution.py:236
  482.8 0.8 slice_reduce_fusion
  483.7 1.0 slice.18
  484.7 0.2 reshape.166
  484.8 0.2 copy.30
  485.0 0.3 fusion.17
  485.3 0.5 add_sqrt_fusion
  485.8 0.1 copy.32
  485.9 0.1 rsqrt.22
  486.0 12.1 %fusion.26 = (f32[16]{0:T(128)S(1)}, f32[16,2400]{1,0:T(8,128)}) fusion(bf16[2400,5120]{1,0:T(8,128)(2,1)} %param.31, f32[16,5120]{1,0:T(8,128)S(1)} %bitcast.48, f32[5120]{0:T(1024)S(1)} %copy-done.9, f32[16]{0:T(128)S(1)} %rsqrt.22), kind=kOutput, calls=%fused_computation.70 | convolution fusion | flops 393500160 | bytes 25077888 | tf_op jit(solution)/shard_map/dot_general | solution.py:395
  498.1 0.7 broadcast_in_dim.108.x_ref
  498.7 11.0 %shard_map.194 = f32[16,128]{1,0:T(8,128)} custom-call(f32[16,128]{1,0:T(8,128)} %broadcast_in_dim.108.x_ref), custom_call_target="tpu_custom_call" | custom-call | tf_op jit(solution)/shard_map/pallas_call | solution.py:236
  509.8 0.8 slice_reduce_fusion.1
  510.6 0.7 reshape_squeeze.7
  (55 shorter events, 0.6 us)
Async XLA Ops:
  7.2 119.4 %copy-start = (s32[4,4]{1,0:T(4,128)S(1)}, s32[4,4]{1,0:T(4,128)}, u32[]{:S(2)}) copy-start(s32[4,4]{1,0:T(4,128)} %param.18) | copy-start | bytes 196
  7.2 63.8 %copy-start.12 = (bf16[2560,256]{1,0:T(8,128)(2,1)S(1)}, bf16[2560,256]{1,0:T(8,128)(2,1)}, u32[]{:S(2)}) copy-start(bf16[2560,256]{1,0:T(8,128)(2,1)} %param.24) | copy-start | bytes 3932164
  7.2 63.8 %copy-start.13 = (bf16[2560,256]{1,0:T(8,128)(2,1)S(1)}, bf16[2560,256]{1,0:T(8,128)(2,1)}, u32[]{:S(2)}) copy-start(bf16[2560,256]{1,0:T(8,128)(2,1)} %param.23) | copy-start | bytes 3932164
  7.2 63.8 %all-gather.6.cloned.1.call-start = ((), (), s32[]{:S(2)}) async-start(), calls=%async_computation.4 | async-start | bytes 3276800 | tf_op jit(solution)/shard_map/all_gather | solution.py:296
  13.5 112.6 %all-gather.8.cloned.1.call-start = ((), (), s32[]{:S(2)}) async-start(), calls=%async_computation.5 | async-start | bytes 9437184 | tf_op jit(solution)/shard_map/all_gather | solution.py:300
  16.0 123.9 %reduce-scatter.5.cloned.1.call-start = ((), (), s32[]{:S(2)}) async-start(), calls=%async_computation.6 | async-start | bytes 5505024 | tf_op jit(solution)/shard_map/reduce_scatter | solution.py:304
  81.5 44.7 %copy-start.11 = (s32[4,512]{1,0:T(4,128)S(1)}, s32[4,512]{1,0:T(4,128)}, u32[]{:S(2)}) copy-start(s32[4,512]{1,0:T(4,128)} %param.17) | copy-start | bytes 24580
  126.1 18.3 %copy-start.5 = (s32[32]{0:T(128)S(1)}, s32[32]{0:T(128)}, u32[]{:S(2)}) copy-start(s32[32]{0:T(128)} %table_ref.1) | copy-start | bytes 388
  126.1 86.2 %all-gather.10.cloned.1.call-start = ((), (), s32[]{:S(2)}) async-start(), calls=%async_computation.7 | async-start | bytes 1966080 | tf_op jit(solution)/shard_map/all_gather | solution.py:332
  128.9 15.5 %copy-start.3 = (f32[256,128]{1,0:T(8,128)S(1)}, f32[256,128]{1,0:T(8,128)}, u32[]{:S(2)}) copy-start(f32[256,128]{1,0:T(8,128)} %get-tuple-element.20.cos_ref) | copy-start | bytes 393220
  128.9 15.5 %copy-start.4 = (f32[256,128]{1,0:T(8,128)S(1)}, f32[256,128]{1,0:T(8,128)}, u32[]{:S(2)}) copy-start(f32[256,128]{1,0:T(8,128)} %get-tuple-element.21.sin_ref) | copy-start | bytes 393220
  139.9 4.5 copy-start.2
  193.0 81.1 %copy-start.6 = (bf16[1,128,2560]{2,1,0:T(8,128)(2,1)S(1)}, bf16[1,128,2560]{2,1,0:T(8,128)(2,1)}, u32[]{:S(2)}) copy-start(bf16[1,128,2560]{2,1,0:T(8,128)(2,1)} %param.16) | copy-start | bytes 1966084
  193.0 81.0 %reduce-scatter.7.cloned.1.call-start = ((), (), s32[]{:S(2)}) async-start(), calls=%async_computation.8 | async-start | bytes 3276800 | tf_op jit(solution)/shard_map/reduce_scatter | solution.py:336
  220.6 57.3 %copy-start.10 = (f32[2560]{0:T(1024)S(1)}, f32[2560]{0:T(1024)}, u32[]{:S(2)}) copy-start(f32[2560]{0:T(1024)} %param.26) | copy-start | bytes 30724
  220.7 114.2 %all-gather.12.cloned.1.call-start = ((), (), s32[]{:S(2)}) async-start(), calls=%async_computation.9 | async-start | bytes 3276800 | tf_op jit(solution)/shard_map/all_gather | solution.py:346
  280.2 95.2 %reduce-scatter.9.cloned.1.call-start = ((), (), s32[]{:S(2)}) async-start(), calls=%async_computation.10 | async-start | bytes 11010048 | tf_op jit(solution)/shard_map/reduce_scatter | solution.py:350
  360.6 34.2 %all-gather.14.cloned.1.call-start = ((), (), s32[]{:S(2)}) async-start(), calls=%async_computation.11 | async-start | bytes 5505024 | tf_op jit(solution)/shard_map/all_gather | solution.py:355
  380.6 30.1 %copy-start.8 = (bf16[256,512]{1,0:T(8,128)(2,1)S(1)}, bf16[256,512]{1,0:T(8,128)(2,1)}, u32[]{:S(2)}) copy-start(bf16[256,512]{1,0:T(8,128)(2,1)} %shard_map.191) | copy-start | bytes 786436
  380.6 83.3 %copy-start.7 = (bf16[128,2560]{1,0:T(8,128)(2,1)S(1)}, bf16[128,2560]{1,0:T(8,128)(2,1)}, u32[]{:S(2)}) copy-start(bf16[128,2560]{1,0:T(8,128)(2,1)} %reduce-scatter.7.cloned.1.call-done) | copy-start | bytes 1966084
  380.6 83.3 %reduce-scatter.11.cloned.1.call-start = ((), (), s32[]{:S(2)}) async-start(), calls=%async_computation.12 | async-start | bytes 3276800 | tf_op jit(solution)/shard_map/reduce_scatter | solution.py:359
  465.4 20.6 %copy-start.9 = (f32[5120]{0:T(1024)S(1)}, f32[5120]{0:T(1024)}, u32[]{:S(2)}) copy-start(f32[5120]{0:T(1024)} %param.30) | copy-start | bytes 61444
  486.0 25.3 %copy-start.1 = (s32[4,4]{1,0:T(4,128)S(1)}, s32[4,4]{1,0:T(4,128)}, u32[]{:S(2)}) copy-start(s32[4,4]{1,0:T(4,128)} %param.18) | copy-start | bytes 196
Sparse Core Ops, SparseCore 0:
  13.6 57.3 all-gather.5
  72.9 53.1 all-gather.7
  128.3 11.5 reduce-scatter.4
  193.2 19.1 all-gather.9
  220.8 53.2 reduce-scatter.6
  280.3 54.4 all-gather.11
  360.7 14.6 reduce-scatter.8
  380.7 14.0 all-gather.13
  410.6 53.2 reduce-scatter.10

commit v2 on v1

--- a/solution.py
+++ b/solution.py
@@ -251,6 +251,109 @@
             collective_id=1 if summing else 2, has_side_effects=True
         ),
     )(values)
+
+
+def gather_body(
+    sizes, x_ref, pages_ref, x_out, pages_out,
+    own_sem, tok_send, tok_recv, grp_send, grp_recv, mdl_send, mdl_recv,
+):
+    grp_n, tok_n, mdl_n = sizes
+    g, t, m = (lax.axis_index(name) for name in ("grp", "tok", "mdl"))
+    grp_peers = [{"grp": lax.rem(g + d, grp_n)} for d in range(1, grp_n)]
+    tok_peers = [{"tok": lax.rem(t + d, tok_n)} for d in range(1, tok_n)]
+    mdl_peers = [{"mdl": lax.rem(m + d, mdl_n)} for d in range(1, mdl_n)]
+    barrier = pltpu.get_barrier_semaphore()
+    for peer in grp_peers + tok_peers + mdl_peers:
+        pl.semaphore_signal(barrier, inc=1, device_id=peer, device_id_type=MESH)
+    pl.semaphore_wait(barrier, grp_n + tok_n + mdl_n - 3)
+
+    def send(source, target, send_sem, recv_sem, peer):
+        copy = pltpu.make_async_remote_copy(
+            src_ref=source,
+            dst_ref=target,
+            send_sem=send_sem,
+            recv_sem=recv_sem,
+            device_id=peer,
+            device_id_type=MESH,
+        )
+        copy.start()
+        return copy
+
+    from_grp = [
+        send(pages_ref, pages_out.at[g, m], grp_send.at[d], grp_recv.at[d], peer)
+        for d, peer in enumerate(grp_peers)
+    ]
+    from_tok = [
+        send(x_ref, x_out.at[t], tok_send.at[d], tok_recv.at[d], peer)
+        for d, peer in enumerate(tok_peers)
+    ]
+    from_mdl = [
+        send(pages_ref, pages_out.at[g, m], mdl_send.at[0, d], mdl_recv.at[0, d], peer)
+        for d, peer in enumerate(mdl_peers)
+    ]
+    own = [
+        pltpu.make_async_copy(x_ref, x_out.at[t], own_sem.at[0]),
+        pltpu.make_async_copy(pages_ref, pages_out.at[g, m], own_sem.at[1]),
+    ]
+    for copy in own:
+        copy.start()
+    for d, copy in enumerate(from_grp):
+        copy.wait_recv()
+        held = pages_out.at[lax.rem(g + grp_n - 1 - d, grp_n), m]
+        for e, peer in enumerate(mdl_peers):
+            from_mdl.append(send(held, held, mdl_send.at[d + 1, e], mdl_recv.at[d + 1, e], peer))
+    for copy in own:
+        copy.wait()
+    for copy in from_grp:
+        copy.wait_send()
+    for copy in from_tok + from_mdl:
+        copy.wait()
+
+
+def gather_rows_and_pages(x, pages):
+    sizes = tuple(lax.axis_size(name) for name in ("grp", "tok", "mdl"))
+    grp_n, tok_n, mdl_n = sizes
+    anywhere = pl.BlockSpec(memory_space=pl.ANY)
+    dma = pltpu.SemaphoreType.DMA
+    rows, all_pages = pl.pallas_call(
+        functools.partial(gather_body, sizes),
+        out_shape=(
+            jax.ShapeDtypeStruct((tok_n,) + x.shape, x.dtype),
+            jax.ShapeDtypeStruct((grp_n, mdl_n) + pages.shape, pages.dtype),
+        ),
+        in_specs=[anywhere, anywhere],
+        out_specs=(anywhere, anywhere),
+        scratch_shapes=[
+            dma((2,)),
+            dma((tok_n,)), dma((tok_n,)),
+            dma((grp_n,)), dma((grp_n,)),
+            dma((grp_n, mdl_n)), dma((grp_n, mdl_n)),
+        ],
+        compiler_params=pltpu.CompilerParams(collective_id=3, has_side_effects=True),
+    )(x, pages)
+    return rows.reshape(-1, x.shape[1]), all_pages.reshape(-1, pages.shape[1])
+
+
+def swap_cores(x):
+    return lax.ppermute(x, "mdl", [(0, 1), (1, 0)])
+
+
+def gather_mdl(x):
+    if lax.axis_size("mdl") != 2:
+        return lax.all_gather(x, "mdl", axis=0, tiled=True)
+    other = swap_cores(x)
+    first = lax.axis_index("mdl") == 0
+    return jnp.concatenate([jnp.where(first, x, other), jnp.where(first, other, x)], 0)
+
+
+def scatter_mdl(x):
+    if lax.axis_size("mdl") != 2:
+        return lax.psum_scatter(x, "mdl", scatter_dimension=0, tiled=True).astype(jnp.float32)
+    rows = x.shape[0] // 2
+    m = lax.axis_index("mdl")
+    theirs = swap_cores(lax.dynamic_slice_in_dim(x, (1 - m) * rows, rows))
+    mine = lax.dynamic_slice_in_dim(x, m * rows, rows)
+    return mine.astype(jnp.float32) + theirs.astype(jnp.float32)
 
 
 def on_device(
@@ -292,16 +395,15 @@
         jnp.bfloat16
     )
     w_joined = jnp.concatenate([w_query, w_key, w_value], 1)
+    all_normed, pages = gather_rows_and_pages(
+        normed, prefix_cache.reshape(-1, kv_dev * 2 * head_dim)
+    )
     partial_qkv = jnp.dot(
-        lax.all_gather(normed, "tok", axis=0, tiled=True),
+        all_normed,
         w_joined,
         preferred_element_type=jnp.float32,
     )
-    pages = lax.all_gather(
-        prefix_cache.reshape(-1, kv_dev * 2 * head_dim), ("grp", "mdl"), axis=0, tiled=True
-    )
-    partial_qkv, pages = lax.optimization_barrier((partial_qkv, pages))
-    qkv_rows = lax.psum_scatter(partial_qkv, "mdl", scatter_dimension=0, tiled=True)
+    qkv_rows = scatter_mdl(partial_qkv)
     seg_row = lax.dynamic_index_in_dim(seg_ids, group_idx, 0, keepdims=False)
     prefix_row = lax.dynamic_index_in_dim(request_prefix, group_idx, 0, keepdims=False)
     requests = jnp.arange(req_count, dtype=jnp.int32)
@@ -329,7 +431,7 @@
         kv_dev, group_size, head_dim, page_len,
     )
     partial_out = jnp.dot(
-        lax.all_gather(attended, "mdl", axis=0, tiled=True),
+        gather_mdl(attended),
         w_out,
         preferred_element_type=jnp.float32,
     )
@@ -347,12 +449,10 @@
         w_pair,
         preferred_element_type=jnp.float32,
     )
-    summed = lax.psum_scatter(
-        partial_ffn.astype(jnp.bfloat16), "mdl", scatter_dimension=0, tiled=True
-    ).astype(jnp.float32)
+    summed = scatter_mdl(partial_ffn.astype(jnp.bfloat16))
     activated = (jax.nn.silu(summed[:, :ff_dev]) * summed[:, ff_dev:]).astype(jnp.bfloat16)
     partial_down = jnp.dot(
-        lax.all_gather(activated, "mdl", axis=0, tiled=True),
+        gather_mdl(activated),
         w_down,
         preferred_element_type=jnp.float32,
     )

time: 519 us -> 455 us (0.88)
  waiting for transfers between devices: 319 us -> 184 us
  Pallas kernels: 76.6 us -> 143 us
  local copies, waits for them, and re-layouts: 8.64 us -> 14.4 us
    all_gather x4 -> x0, waiting for transfers between devices: 133 us -> none  [the longest x1 55 us: on_device(): lax.all_gather(normed, 'tok', axis=0, tiled=True)]
    pallas_call x0 -> x1, Pallas kernels: none -> 58 us  [gather_rows_and_pages(): pl.pallas_call(functools.partial(gather_body, sizes), out_shape=(jax.Shap...]
    reduce_scatter x2 -> x0, waiting for transfers between devices: 25.8 us -> none  [the longest x1 14.8 us: on_device(): lax.psum_scatter(partial_ffn.astype(jnp.bfloat16), 'mdl', scatter_dimensi...]
    ppermute x0 -> x4, waiting for transfers between devices: none -> 13.4 us  [swap_cores(): return lax.ppermute(x, 'mdl', [(0, 1), (1, 0)])]
    reduce_scatter x1, waiting for transfers between devices: 53.4 us -> 65.8 us  [on_device(): lax.psum_scatter(partial_out.astype(jnp.bfloat16), 'tok', scatter_dimensi...]
    pallas_call x1, Pallas kernels: 48.6 us -> 57.3 us  [attend(): pl.pallas_call(body, grid_spec=pltpu.PrefetchScalarGridSpec(num_scalar_pr...]
  transfers between devices with their start and end apart: 9 -> 7, of which waited for: 9 -> 7; matrix products, arithmetic and copies ran while one was open for 3% -> 1% of each run, Pallas kernels for 0% -> 0%
where the time goes in v2:
time: 455 us; the launch traced here: 454 us
  waiting for transfers between devices  184 us (40%)
  Pallas kernels  143 us (31%)
  matrix products  69.7 us (15%)
  other arithmetic  20.9 us (5%)
  local copies, waits for them, and re-layouts  14.4 us (3%)
  between operations  14.1 us (3%)
  blocking collectives  7.43 us (2%)
    reduce_scatter x1, waiting for transfers between devices, on_device(): lax.psum_scatter(partial_out.astype(jnp.bfloat16), 'tok', scatter_dimensi...  65.8 us
    pallas_call x1, Pallas kernels, gather_rows_and_pages(): pl.pallas_call(functools.partial(gather_body, sizes), out_shape=(jax.Shap...  58 us
    pallas_call x1, Pallas kernels, attend(): pl.pallas_call(body, grid_spec=pltpu.PrefetchScalarGridSpec(num_scalar_pr...  57.3 us
    all_gather x1, waiting for transfers between devices, on_device(): lax.all_gather(ffn_input, 'tok', axis=0, tiled=True)  54.4 us
    reduce_scatter x1, waiting for transfers between devices, on_device(): lax.psum_scatter(partial_down.astype(jnp.bfloat16), 'tok', scatter_dimens...  50.1 us
    pallas_call x2, Pallas kernels, exchange(): pl.pallas_call(functools.partial(exchange_body, sizes, summing), out_shap...  25.9 us
    dot_general x1, matrix products, on_device(): jnp.dot(lax.all_gather(ffn_input, 'tok', axis=0, tiled=True), w_pair, pre...  25.7 us
    dot_general x1, matrix products, on_device(): jnp.dot(gather_mdl(activated), w_down, preferred_element_type=jnp.float32)  14.6 us
  transfers between devices with their start and end apart: 7, of which 7 were waited for; matrix products, arithmetic and copies ran while one was open for 1% of the time, Pallas kernels for 0%

profile of v2, /device:TPU:0, one launch (start us, length us, event | category | flops | bytes accessed | tf_op | source)
XLA Modules:
  0.0 454.3 jit_solution(1269439312233315323)
XLA Ops:
  7.3 1.5 fusion.17
  8.7 2.6 psum.14
  11.3 2.4 copy.31
  13.7 2.1 fusion.19.x_ref
  15.9 58.0 %shard_map.191 = (bf16[4,128,2560]{2,1,0:T(8,128)(2,1)}, bf16[4,2,1024,512]{3,2,1,0:T(8,128)(2,1)}) custom-call(bf16[128,2560]{1,0:T(8,128)(2,1)} %fusion.19.x_ref, bf16[1024,512]{1,0:T(8,128)(2,1)} %bitcast.47), custom_call_target="tpu_custom_call" | custom-call | tf_op jit(solution)/shard_map/pallas_call | solution.py:318
  73.9 9.2 %fusion.7 = f32[512,1792]{1,0:T(8,128)S(1)} fusion(bf16[512,2560]{1,0:T(8,128)(2,1)} %bitcast.57, bf16[2560,256]{1,0:T(8,128)(2,1)S(1)} %copy-done.14, bf16[2560,256]{1,0:T(8,128)(2,1)S(1)} %copy-done.15, bf16[2560,1280]{1,0:T(8,128)(2,1)} %param.22), kind=kOutput, calls=%fused_computation.5 | convolution fusion | flops 4725145600 | bytes 15466496 | tf_op jit(solution)/shard_map/dot_general | solution.py:401
  83.1 1.9 copy-done.9
  85.0 1.5 constant_dynamic-slice_fusion.2
  86.4 0.1 convert_reduce_fusion
  86.5 0.2 reduce-window.7
  86.8 0.1 select_reduce_fusion.1
  86.9 0.1 eq.86
  87.0 0.1 convert_reduce_fusion.1
  87.1 0.1 copy.26
  87.2 0.1 reshape.166.need_ref
  87.4 0.1 copy.27.seg_ref
  87.5 0.1 copy.28.prefix_ref
  87.7 0.5 fusion.27
  88.3 0.8 pad_maximum_fusion
  89.1 1.3 collective-permute-done
  90.4 3.0 dynamic-slice_add_fusion.k_ref.v_ref.q_ref
  93.4 2.2 shard_map.192
  95.6 2.4 all_gather.6.suffix_ref
  98.0 57.3 %shard_map.193 = bf16[256,1280]{1,0:T(8,128)(2,1)S(1)} custom-call(s32[32]{0:T(128)S(1)} %copy-done.5, s32[8]{0:T(128)S(1)} %reshape.166.need_ref, f32[256,1792]{1,0:T(8,128)S(1)} %copy-done.2, f32[256,128]{1,0:T(8,128)S(1)} %copy-done.3, f32[256,128]{1,0:T(8,128)S(1)} %copy-done.4, s32[256,1]{1,0:T(8,128)S(1)} %copy.27.seg_ref, ...), custom_call_target="tpu_custom_call" | custom-call | flops 6039797760 | bytes 8388608 | tf_op jit(solution)/shard_map/pallas_call | solution.py:152
  155.4 2.1 collective-permute-done.1
  157.5 0.1 broadcast_select_fusion.3
  157.6 8.2 %convolution_convert_fusion.1 = bf16[512,2560]{1,0:T(8,128)(2,1)} fusion(bf16[1280,2560]{1,0:T(8,128)(2,1)} %param.25, bf16[256,1280]{1,0:T(8,128)(2,1)S(1)} %get-tuple-element.16, bf16[256,1280]{1,0:T(8,128)(2,1)S(1)} %get-tuple-element.15), kind=kOutput, calls=%fused_computation.14 | convolution fusion | flops 3359375360 | bytes 10485760 | tf_op jit(solution)/shard_map/dot_general | solution.py:433
  165.8 65.8 %reduce-scatter.3.cloned.1.call-done = bf16[128,2560]{1,0:T(8,128)(2,1)} async-done(((bf16[512,2560]{1,0:T(8,128)(2,1)}), bf16[128,2560]{1,0:T(8,128)(2,1)}) %reduce-scatter.3.cloned.1.call-update) | async-done | bytes 655376 | tf_op jit(solution)/shard_map/reduce_scatter | solution.py:438
  231.6 1.4 multiply_reduce_fusion.1
  233.0 2.5 psum.15
  235.5 2.2 multiply_convert_fusion
  237.7 0.2 reduce-scatter.5.cloned.1.call-start
  238.0 54.4 %all-gather.2.cloned.1.call-done = bf16[512,2560]{1,0:T(8,128)(2,1)} async-done(((bf16[128,2560]{1,0:T(8,128)(2,1)}), bf16[512,2560]{1,0:T(8,128)(2,1)}) %all-gather.2.cloned.1.call-update) | async-done | bytes 2621456 | tf_op jit(solution)/shard_map/all_gather | solution.py:448
  292.4 25.7 %fusion.4 = bf16[512,7168]{1,0:T(8,128)(2,1)} fusion(bf16[512,2560]{1,0:T(8,128)(2,1)} %all-gather.2.cloned.1.call-done, bf16[2560,3584]{1,0:T(8,128)(2,1)} %param.28, bf16[2560,3584]{1,0:T(8,128)(2,1)} %param.27), kind=kOutput, calls=%fused_computation.4 | convolution fusion | flops 18867552256 | bytes 46661632 | tf_op jit(solution)/shard_map/dot_general | solution.py:447
  318.1 2.4 constant_dynamic-slice_fusion
  320.6 6.4 %collective-permute-done.2 = bf16[256,7168]{1,0:T(8,128)(2,1)S(1)} collective-permute-done((bf16[256,7168]{1,0:T(8,128)(2,1)S(1)}, bf16[256,7168]{1,0:T(8,128)(2,1)S(1)}, u32[]{:S(2)}, u32[]{:S(2)}) %collective-permute-start.2) | collective-permute-done | bytes 3670048 | tf_op jit(solution)/shard_map/ppermute | solution.py:338
  327.0 1.2 convert_add_fusion
  328.2 1.1 fusion.13
  329.3 0.2 collective-permute-start.3
  329.5 3.6 collective-permute-done.3
  333.2 1.6 broadcast_select_fusion.1
  334.8 14.6 %convolution_convert_fusion = bf16[512,2560]{1,0:T(8,128)(2,1)} fusion(bf16[3584,2560]{1,0:T(8,128)(2,1)} %param.29, bf16[256,3584]{1,0:T(8,128)(2,1)S(1)} %get-tuple-element.14, bf16[256,3584]{1,0:T(8,128)(2,1)S(1)} %get-tuple-element.13), kind=kOutput, calls=%fused_computation.13 | convolution fusion | flops 9403891712 | bytes 24641536 | tf_op jit(solution)/shard_map/dot_general | solution.py:454
  349.4 0.1 dynamic-slice_bitcast_fusion
  349.6 0.8 reshape.172
  350.3 50.1 %reduce-scatter.5.cloned.1.call-done = bf16[128,2560]{1,0:T(8,128)(2,1)} async-done(((bf16[512,2560]{1,0:T(8,128)(2,1)}), bf16[128,2560]{1,0:T(8,128)(2,1)}) %reduce-scatter.5.cloned.1.call-update) | async-done | bytes 655376 | tf_op jit(solution)/shard_map/reduce_scatter | solution.py:459
  400.4 1.5 multiply_reduce_fusion
  401.9 0.1 select_reduce_fusion.3
  402.0 0.1 copy.29
  402.1 0.9 convert_bitcast_fusion
  403.0 0.7 select_reduce_fusion
  403.8 0.6 select_maximum_fusion.x_ref
  404.4 14.9 %shard_map.194 = f32[8,8,1408]{2,1,0:T(8,128)} custom-call(f32[8,1408]{1,0:T(8,128)} %select_maximum_fusion.x_ref), custom_call_target="tpu_custom_call" | custom-call | tf_op jit(solution)/shard_map/pallas_call | solution.py:236
  419.3 0.8 slice_reduce_fusion
  420.1 1.0 slice.18
  421.1 0.2 reshape.174
  421.3 0.3 fusion.23
  421.6 0.2 copy.30
  421.8 0.5 add_sqrt_fusion
  422.4 0.1 rsqrt.22
  422.5 12.1 %fusion.34 = (f32[16]{0:T(128)S(1)}, f32[16,2400]{1,0:T(8,128)}) fusion(bf16[2400,5120]{1,0:T(8,128)(2,1)} %param.31, f32[16,5120]{1,0:T(8,128)S(1)} %bitcast.48, f32[5120]{0:T(1024)S(1)} %copy-done.11, f32[16]{0:T(128)S(1)} %rsqrt.22), kind=kOutput, calls=%fused_computation.86 | convolution fusion | flops 393500160 | bytes 25077888 | tf_op jit(solution)/shard_map/dot_general | solution.py:495
  434.5 0.7 broadcast_in_dim.108.x_ref
  435.2 11.0 %shard_map.195 = f32[16,128]{1,0:T(8,128)} custom-call(f32[16,128]{1,0:T(8,128)} %broadcast_in_dim.108.x_ref), custom_call_target="tpu_custom_call" | custom-call | tf_op jit(solution)/shard_map/pallas_call | solution.py:236
  446.3 0.8 slice_reduce_fusion.1
  447.1 0.7 reshape_squeeze.7
  (55 shorter events, 0.8 us)
Async XLA Ops:
  7.2 79.6 %copy-start = (s32[4,4]{1,0:T(4,128)S(1)}, s32[4,4]{1,0:T(4,128)}, u32[]{:S(2)}) copy-start(s32[4,4]{1,0:T(4,128)} %param.18) | copy-start | bytes 196
  7.2 66.7 %copy-start.14 = (bf16[2560,256]{1,0:T(8,128)(2,1)S(1)}, bf16[2560,256]{1,0:T(8,128)(2,1)}, u32[]{:S(2)}) copy-start(bf16[2560,256]{1,0:T(8,128)(2,1)} %param.24) | copy-start | bytes 3932164
  7.2 66.7 %copy-start.15 = (bf16[2560,256]{1,0:T(8,128)(2,1)S(1)}, bf16[2560,256]{1,0:T(8,128)(2,1)}, u32[]{:S(2)}) copy-start(bf16[2560,256]{1,0:T(8,128)(2,1)} %param.23) | copy-start | bytes 3932164
  7.2 224.4 %reduce-scatter.3.cloned.1.call-start = ((), (), s32[]{:S(2)}) async-start(), calls=%async_computation.2 | async-start | bytes 3276800 | tf_op jit(solution)/shard_map/reduce_scatter | solution.py:438
  83.1 1.9 copy-start.9
  85.0 1.5 copy-start.13
  86.4 4.0 collective-permute-start
  93.4 4.6 %copy-start.2 = (f32[256,1792]{1,0:T(8,128)S(1)}, f32[256,1792]{1,0:T(8,128)}, u32[]{:S(2)}) copy-start(f32[256,1792]{1,0:T(8,128)} %dynamic-slice_add_fusion.k_ref.v_ref.q_ref) | copy-start | bytes 5505028
  93.4 4.6 %copy-start.3 = (f32[256,128]{1,0:T(8,128)S(1)}, f32[256,128]{1,0:T(8,128)}, u32[]{:S(2)}) copy-start(f32[256,128]{1,0:T(8,128)} %get-tuple-element.24.cos_ref) | copy-start | bytes 393220
  93.4 4.6 %copy-start.4 = (f32[256,128]{1,0:T(8,128)S(1)}, f32[256,128]{1,0:T(8,128)}, u32[]{:S(2)}) copy-start(f32[256,128]{1,0:T(8,128)} %get-tuple-element.25.sin_ref) | copy-start | bytes 393220
  93.4 4.6 %copy-start.5 = (s32[32]{0:T(128)S(1)}, s32[32]{0:T(128)}, u32[]{:S(2)}) copy-start(s32[32]{0:T(128)} %table_ref.1) | copy-start | bytes 388
  155.3 2.2 collective-permute-start.1
  157.6 74.0 %copy-start.6 = (bf16[1,128,2560]{2,1,0:T(8,128)(2,1)S(1)}, bf16[1,128,2560]{2,1,0:T(8,128)(2,1)}, u32[]{:S(2)}) copy-start(bf16[1,128,2560]{2,1,0:T(8,128)(2,1)} %param.16) | copy-start | bytes 1966084
  165.8 69.7 %copy-start.12 = (f32[2560]{0:T(1024)S(1)}, f32[2560]{0:T(1024)}, u32[]{:S(2)}) copy-start(f32[2560]{0:T(1024)} %param.26) | copy-start | bytes 30724
  165.8 126.6 %all-gather.2.cloned.1.call-start = ((), (), s32[]{:S(2)}) async-start(), calls=%async_computation.3 | async-start | bytes 3276800 | tf_op jit(solution)/shard_map/all_gather | solution.py:448
  237.7 162.7 %reduce-scatter.5.cloned.1.call-start = ((), (), s32[]{:S(2)}) async-start(), calls=%async_computation.4 | async-start | bytes 3276800 | tf_op jit(solution)/shard_map/reduce_scatter | solution.py:459
  318.1 8.9 %copy-start.7 = (bf16[512,7168]{1,0:T(8,128)(2,1)S(1)}, bf16[512,7168]{1,0:T(8,128)(2,1)}, u32[]{:S(2)}) copy-start(bf16[512,7168]{1,0:T(8,128)(2,1)} %fusion.4) | copy-start | bytes 22020100
  320.5 6.5 %collective-permute-start.2 = (bf16[256,7168]{1,0:T(8,128)(2,1)S(1)}, bf16[256,7168]{1,0:T(8,128)(2,1)S(1)}, u32[]{:S(2)}, u32[]{:S(2)}) collective-permute-start(bf16[256,7168]{1,0:T(8,128)(2,1)S(1)} %constant_dynamic-slice_fusion), channel_id=1, source_target_pairs={{0,1},{1,0},{2,3},{3,2},{4,5},{5,4},{6,7},{7,6},{8,9},{9,8},{10,11... | collective-permute-start | bytes 11010056 | tf_op jit(solution)/shard_map/ppermute | solution.py:338
  329.3 3.9 collective-permute-start.3
  334.7 14.8 %copy-start.10 = (bf16[256,512]{1,0:T(8,128)(2,1)S(1)}, bf16[256,512]{1,0:T(8,128)(2,1)}, u32[]{:S(2)}) copy-start(bf16[256,512]{1,0:T(8,128)(2,1)} %shard_map.192) | copy-start | bytes 786436
  334.8 65.7 %copy-start.8 = (bf16[128,2560]{1,0:T(8,128)(2,1)S(1)}, bf16[128,2560]{1,0:T(8,128)(2,1)}, u32[]{:S(2)}) copy-start(bf16[128,2560]{1,0:T(8,128)(2,1)} %reduce-scatter.3.cloned.1.call-done) | copy-start | bytes 1966084
  401.9 20.6 %copy-start.11 = (f32[5120]{0:T(1024)S(1)}, f32[5120]{0:T(1024)}, u32[]{:S(2)}) copy-start(f32[5120]{0:T(1024)} %param.30) | copy-start | bytes 61444
  422.5 25.3 %copy-start.1 = (s32[4,4]{1,0:T(4,128)S(1)}, s32[4,4]{1,0:T(4,128)}, u32[]{:S(2)}) copy-start(s32[4,4]{1,0:T(4,128)} %param.18) | copy-start | bytes 196
Sparse Core Ops, SparseCore 0:
  165.9 65.6 reduce-scatter.2
  237.8 54.4 all-gather.1
  349.5 50.8 reduce-scatter.4
